TPU v7x, 128 devices: a whole 4x4x4 slice. The times are simulated.
128 devices in a mesh: row: 4 (over z_hi, core), col: 32 (over x, y, z_lo).
Axes of the slice: x: 4, y: 4, z: 4 (z_hi: 2, z_lo: 2; z = z_hi * 2 + z_lo), core: 2. Of those that a mesh axis runs over, the one named last changes fastest.
Arguments:
- node_features: float32 [32768, 256], P(('col', 'row')), may hold values from -6 to 6
- self_weight: float32 [256, 256], replicated, may hold values from -0.375 to 0.375
- neighbour_weight: float32 [256, 256], replicated, may hold values from -0.375 to 0.375
- layer_bias: float32 [256], replicated, may hold values from -3 to 3
- tile_values: float32 [4, 32, 192, 128, 128], P('row', 'col'), as said below
- tile_dest: int32 [4, 32, 192], P('row', 'col'), may hold values from 0 to 63
- tile_source: int32 [4, 32, 192], P('row', 'col'), may hold values from 0 to 7
- tile_count: int32 [4, 32], P('row', 'col'), may hold values from 48 to 192, as said below
- cotangent: float32 [32768, 256], P(('col', 'row')), may hold values from -6 to 6
Outputs:
- layer_out: float32 [32768, 256], P(('col', 'row'))
- grad_features: float32 [32768, 256], P(('col', 'row'))
- grad_self_weight: float32 [256, 256], replicated
- grad_neighbour_weight: float32 [256, 256], replicated
- grad_bias: float32 [256], replicated
Inputs may be any that keep to these rules, and one draw needn't show every extreme that they name: `tile_count`: list positions at or past a device's count are unused; some device lists exactly 192 tiles. `tile_values`: Non-negative edge weights.
All inputs are finite; a program needn't handle non-finite values.
Results may differ from a plain program's by a relative error of at most 0.0003.
Values sent between devices are 32-bit elements; how exact they have to be, the bound alone decides.
A program may use at most 192 MiB of HBM per device.

v0:
```python
import jax
import jax.numpy as jnp
from jax import lax
from jax.sharding import PartitionSpec as P

EPSILON = 1e-05
HIGHEST = lax.Precision.HIGHEST


def finish(pre_act):
    activated = jax.nn.silu(pre_act)
    return activated * lax.rsqrt(jnp.mean(activated * activated, axis=-1, keepdims=True) + EPSILON)


def one_hot_rows(labels, extent, live_mask):
    return (labels[None, :] == jnp.arange(extent)[:, None]).astype(jnp.float32) * live_mask[None, :]


def tile_products(values, picked):
    return jnp.einsum("tij,tjf->tif", values, picked, precision=HIGHEST)


def tile_backs(values, picked):
    return jnp.einsum("tij,tif->tjf", values, picked, precision=HIGHEST)


def body(
    node_features,
    self_weight,
    neighbour_weight,
    layer_bias,
    tile_values,
    tile_dest,
    tile_source,
    tile_count,
    cotangent,
):
    slot_total = tile_values.shape[2]
    tile_side = tile_values.shape[3]
    feature_width = node_features.shape[1]
    own_count = node_features.shape[0] // tile_side
    dest_total = own_count * lax.axis_size("col")
    source_total = own_count * lax.axis_size("row")
    flat_width = tile_side * feature_width
    values = tile_values.reshape(slot_total, tile_side, tile_side)
    dest_ids = tile_dest.reshape(slot_total)
    source_ids = tile_source.reshape(slot_total)
    list_count = tile_count.reshape(())
    slot_ids = jnp.arange(slot_total)
    own_blocks = node_features.reshape(own_count, tile_side, feature_width)
    slab = lax.all_gather(own_blocks, "row", axis=0, tiled=True)
    home_mask = (slot_ids < list_count).astype(jnp.float32)
    products = tile_products(values, slab[source_ids])
    dest_hot = one_hot_rows(dest_ids, dest_total, home_mask)
    partial_sum = jnp.dot(dest_hot, products.reshape(slot_total, flat_width), precision=HIGHEST)
    partial_degree = jnp.dot(dest_hot, jnp.sum(values, axis=2), precision=HIGHEST)
    summed, degree = (
        lax.psum_scatter(partial_sum, "col", scatter_dimension=0, tiled=True),
        lax.psum_scatter(partial_degree, "col", scatter_dimension=0, tiled=True),
    )
    inv_root = lax.rsqrt(1.0 + degree.reshape(own_count * tile_side, 1))
    neighbour = summed.reshape(own_count * tile_side, feature_width) * inv_root
    pre_act = (
        jnp.dot(node_features, self_weight, precision=HIGHEST)
        + jnp.dot(neighbour, neighbour_weight, precision=HIGHEST)
        + layer_bias
    )
    layer_out, pullback = jax.vjp(finish, pre_act)
    grad_pre = pullback(cotangent)[0]
    grad_self_weight, grad_neighbour_weight, grad_bias = lax.psum(
        (
            jnp.dot(node_features.T, grad_pre, precision=HIGHEST),
            jnp.dot(neighbour.T, grad_pre, precision=HIGHEST),
            jnp.sum(grad_pre, axis=0),
        ),
        ("row", "col"),
    )
    outgoing = jnp.dot(grad_pre, neighbour_weight.T, precision=HIGHEST) * inv_root
    gathered = lax.all_gather(
        outgoing.reshape(own_count, tile_side, feature_width), "col", axis=0, tiled=True
    )
    back_terms = tile_backs(values, gathered[dest_ids])
    source_hot = one_hot_rows(source_ids, source_total, home_mask)
    partial_back = jnp.dot(
        source_hot, back_terms.reshape(slot_total, flat_width), precision=HIGHEST
    )
    reduced = lax.psum_scatter(partial_back, "row", scatter_dimension=0, tiled=True).reshape(
        own_count * tile_side, feature_width
    )
    grad_features = jnp.dot(grad_pre, self_weight.T, precision=HIGHEST) + reduced
    return (layer_out, grad_features, grad_self_weight, grad_neighbour_weight, grad_bias)


def solution(mesh):
    in_specs = (
        P(("col", "row"), None),
        P(),
        P(),
        P(),
        P("row", "col", None, None, None),
        P("row", "col", None),
        P("row", "col", None),
        P("row", "col"),
        P(("col", "row"), None),
    )
    out_specs = (P(("col", "row"), None), P(("col", "row"), None), P(), P(), P())
    return jax.shard_map(body, mesh=mesh, in_specs=in_specs, out_specs=out_specs, check_vma=False)
```

profile of v0, /device:TPU:1, one launch (start us, length us, event | category | flops | bytes accessed | tf_op | source)
XLA Modules:
  0.0 926.2 jit_solution(15275742767277620158)
XLA Ops:
  7.2 0.0 copy-start
  7.2 0.0 all-gather.3.cloned.1.call-start
  7.2 0.7 all-gather.3.cloned.1.call-update
  7.9 0.0 all-reduce.8.cloned.1.call-start
  8.6 0.7 compare_select_fusion.1
  9.3 24.9 %all-gather.3.cloned.1.call-done = f32[8,128,256]{2,1,0:T(8,128)} async-done(((f32[2,128,256]{2,1,0:T(8,128)}), f32[8,128,256]{2,1,0:T(8,128)}) %all-gather.3.cloned.1.call-update) | async-done | bytes 1048592 | tf_op jit(solution)/shard_map/all_gather | solution.py:51
  34.2 13.5 %gather_fusion = f32[192,128,256]{2,1,0:T(8,128)} fusion(f32[8,128,256]{2,1,0:T(8,128)} %all-gather.3.cloned.1.call-done, s32[1024]{0:T(1024)S(1)} %pad_clamp_fusion.1), kind=kCustom, calls=%fused_computation | custom fusion | bytes 50332416 | tf_op jit(solution)/shard_map/gather | solution.py:53
  47.7 49.1 %fusion.4 = f32[192,128,256]{1,2,0:T(8,128)} fusion(f32[192,128,256]{2,1,0:T(8,128)} %gather_fusion, f32[1,1,192,128,128]{4,3,2,1,0:T(8,128)} %param.13), kind=kOutput, calls=%fused_computation.6 | convolution fusion | flops 9663676416 | bytes 62914560 | tf_op jit(solution)/shard_map/tij,tjf->tif/dot_general | solution.py:20
  96.9 0.0 copy-start.5
  96.9 24.8 %copy.36 = f32[24,8,128,256]{3,1,2,0:T(8,128)} copy(f32[24,8,128,256]{2,3,1,0:T(8,128)} %bitcast.52) | data formatting | bytes 50331648
  121.7 0.0 copy-start.4
  121.7 0.0 copy-done.5
  121.7 0.0 copy-start.9
  121.7 0.0 copy-start.2
  121.7 0.0 copy-start.3
  121.7 0.0 copy-start.7
  121.7 22.6 %fusion.21 = f32[64,32768]{1,0:T(8,128)} fusion(f32[192,32768]{1,0:T(8,128)} %bitcast.55, f32[192]{0:T(256)S(1)} %compare_convert_fusion, s32[192]{0:T(256)S(1)} %bitcast.58), kind=kOutput, calls=%fused_computation.29 | convolution fusion | flops 4831862784 | bytes 33555968 | tf_op jit(solution)/shard_map/dot_general | solution.py:55
  144.3 0.0 all-reduce.8.cloned.1.call-update
  144.3 0.0 all-gather.5.cloned.1.call-start
  144.3 0.0 copy-done.4
  144.4 0.1 copy.28
  144.5 7.9 reduce_sum.40
  152.4 0.0 copy-done.9
  152.4 0.6 dynamic-slice
  153.6 0.2 fusion.19
  153.9 134.7 %all-reduce.1 = f32[64,128]{1,0:T(8,128)S(1)} all-reduce(f32[64,128]{1,0:T(8,128)S(1)} %fusion.19), channel_id=3, replica_groups=mesh['row'=4,'col'=32] {'col'}, use_global_device_ids=true, to_apply=%region_2.0.clone | all-reduce | flops 8192 | bytes 65536
  288.6 0.0 copy-done.2
  288.6 0.0 copy-done.3
  288.6 0.6 fusion.42
  289.2 235.3 %all-reduce.8.cloned.1.call-done = f32[64,32768]{1,0:T(8,128)} async-done(((f32[64,32768]{1,0:T(8,128)}), f32[64,32768]{1,0:T(8,128)}) %all-reduce.8.cloned.1.call-update) | async-done | bytes 8388624
  524.5 1.3 constant_dynamic-slice_fusion.1
  525.8 0.2 reshape.138
  526.1 0.0 copy-done
  526.1 0.0 copy-done.7
  526.1 0.7 multiply_reduce_fusion
  526.8 0.2 fusion.40
  527.0 1.3 convolution_multiply_fusion
  528.3 0.0 all-gather.5.cloned.1.call-update
  528.4 0.0 all-reduce.12.cloned.1.call-start
  528.4 1.1 convolution_bitcast_fusion
  529.5 1.4 fusion.14
  530.9 0.0 all-reduce.12.cloned.1.call-update
  530.9 0.0 all-reduce.10.cloned.1.call-start
  531.0 185.4 %all-gather.5.cloned.1.call-done = f32[64,128,256]{2,1,0:T(8,128)} async-done(((f32[2,128,256]{2,1,0:T(8,128)}), f32[64,128,256]{2,1,0:T(8,128)}) %all-gather.5.cloned.1.call-update) | async-done | bytes 8388624 | tf_op jit(solution)/shard_map/all_gather | solution.py:79
  716.4 15.8 %gather_fusion.1 = f32[192,128,256]{2,1,0:T(8,128)} fusion(f32[64,128,256]{2,1,0:T(8,128)} %all-gather.5.cloned.1.call-done, s32[1024]{0:T(1024)S(1)} %pad_clamp_fusion), kind=kCustom, calls=%fused_computation.1 | custom fusion | bytes 50332416 | tf_op jit(solution)/shard_map/gather | solution.py:82
  732.2 49.0 %fusion.7 = f32[192,128,256]{1,2,0:T(8,128)} fusion(f32[192,128,256]{2,1,0:T(8,128)} %gather_fusion.1, f32[1,1,192,128,128]{4,3,2,1,0:T(8,128)} %param.13), kind=kOutput, calls=%fused_computation.7 | convolution fusion | flops 9663676416 | bytes 62914560 | tf_op jit(solution)/shard_map/tij,tif->tjf/dot_general | solution.py:24
  781.2 0.0 copy-start.6
  781.2 0.0 copy-start.1
  781.2 24.9 %copy.37 = f32[24,8,128,256]{3,1,2,0:T(8,128)} copy(f32[24,8,128,256]{2,3,1,0:T(8,128)} %bitcast.53) | data formatting | bytes 50331648
  806.1 0.0 copy-done.6
  806.1 16.6 %fusion.29 = f32[8,32768]{1,0:T(8,128)} fusion(f32[192,32768]{1,0:T(8,128)} %bitcast.54, f32[192]{0:T(256)S(1)} %compare_convert_fusion, s32[192]{0:T(256)S(1)} %bitcast.62), kind=kOutput, calls=%fused_computation.38 | convolution fusion | flops 603982848 | bytes 26215936 | tf_op jit(solution)/shard_map/dot_general | solution.py:84
  822.6 0.0 all-reduce.10.cloned.1.call-update
  822.6 0.0 copy-done.8
  822.7 0.6 dynamic-slice.4
  823.9 0.8 copy.32
  824.7 67.3 %psum.23 = f32[256]{0:T(256)} all-reduce(f32[256]{0:T(256)S(1)} %get-tuple-element.24), channel_id=1, replica_groups=mesh['row'=4,'col'=32] {'row','col'}, use_global_device_ids=true, to_apply=%region_9.10 | all-reduce | flops 256 | bytes 2048 | tf_op jit(solution)/shard_map/psum | solution.py:70
  892.1 0.0 all-reduce.12.cloned.1.call-done
  892.1 1.8 copy.33
  893.9 20.8 %all-reduce.10.cloned.1.call-done = f32[8,32768]{1,0:T(8,128)} async-done(((f32[8,32768]{1,0:T(8,128)}), f32[8,32768]{1,0:T(8,128)}) %all-reduce.10.cloned.1.call-update) | async-done | bytes 1048592
  914.7 1.3 constant_dynamic-slice_fusion
  916.0 0.2 reshape.142
  916.3 1.3 convolution_add_fusion
  917.6 1.7 copy.45
  919.2 0.0 copy-done.1
  (7 shorter events, 0.0 us)
Async XLA Ops:
  7.2 518.9 %copy-start = (f32[256,256]{1,0:T(8,128)S(1)}, f32[256,256]{1,0:T(8,128)}, u32[]{:S(2)}) copy-start(f32[256,256]{1,0:T(8,128)} %param.11) | copy-start | bytes 786436
  7.2 27.1 %all-gather.3.cloned.1.call-start = ((), (), s32[]{:S(2)}) async-start(), calls=%async_computation | async-start | bytes 1310720 | tf_op jit(solution)/shard_map/all_gather | solution.py:51
  7.9 516.6 %all-reduce.8.cloned.1.call-start = ((), (), s32[]{:S(2)}) async-start(), calls=%async_computation.2 | async-start | bytes 16777216
  96.9 24.8 %copy-start.5 = (s32[1,1,192]{2,1,0:T(1,128)S(1)}, s32[1,1,192]{2,1,0:T(1,128)}, u32[]{:S(2)}) copy-start(s32[1,1,192]{2,1,0:T(1,128)} %param.14) | copy-start | bytes 2308
  121.7 22.7 %copy-start.4 = (f32[256,256]{1,0:T(8,128)S(1)}, f32[256,256]{1,0:T(8,128)}, u32[]{:S(2)}) copy-start(f32[256,256]{1,0:T(8,128)} %param.17) | copy-start | bytes 786436
  121.7 30.7 %copy-start.9 = (u32[128]{0:T(128)S(1)}, u32[128]{0:T(128)}, u32[]{:S(2)}) copy-start(u32[128]{0:T(128)} %constant.28) | copy-start | bytes 1540
  121.7 166.9 %copy-start.2 = (f32[256,256]{1,0:T(8,128)S(1)}, f32[256,256]{1,0:T(8,128)}, u32[]{:S(2)}) copy-start(f32[256,256]{1,0:T(8,128)} %param.9) | copy-start | bytes 786436
  121.7 166.9 %copy-start.3 = (f32[256,256]{1,0:T(8,128)S(1)}, f32[256,256]{1,0:T(8,128)}, u32[]{:S(2)}) copy-start(f32[256,256]{1,0:T(8,128)} %param.10) | copy-start | bytes 786436
  121.7 404.4 %copy-start.7 = (f32[256]{0:T(256)S(1)}, f32[256]{0:T(256)}, u32[]{:S(2)}) copy-start(f32[256]{0:T(256)} %param.12) | copy-start | bytes 3076
  144.3 572.1 %all-gather.5.cloned.1.call-start = ((), (), s32[]{:S(2)}) async-start(), calls=%async_computation.1 | async-start | bytes 8650752 | tf_op jit(solution)/shard_map/all_gather | solution.py:79
  528.4 363.8 %all-reduce.12.cloned.1.call-start = ((), (), s32[]{:S(2)}) async-start(), calls=%async_computation.4 | async-start | bytes 1048576 | tf_op jit(solution)/shard_map/psum | solution.py:70
  530.9 383.8 %all-reduce.10.cloned.1.call-start = ((), (), s32[]{:S(2)}) async-start(), calls=%async_computation.3 | async-start | bytes 2097152
  781.2 24.9 %copy-start.6 = (s32[1,1,192]{2,1,0:T(1,128)S(1)}, s32[1,1,192]{2,1,0:T(1,128)}, u32[]{:S(2)}) copy-start(s32[1,1,192]{2,1,0:T(1,128)} %param.15) | copy-start | bytes 2308
  781.2 138.0 %copy-start.1 = (f32[256,256]{1,0:T(8,128)S(1)}, f32[256,256]{1,0:T(8,128)}, u32[]{:S(2)}) copy-start(f32[256,256]{1,0:T(8,128)} %param.11) | copy-start | bytes 786436
  806.1 16.6 %copy-start.8 = (u32[128]{0:T(128)S(1)}, u32[128]{0:T(128)}, u32[]{:S(2)}) copy-start(u32[128]{0:T(128)} %constant.36) | copy-start | bytes 1540
Sparse Core Ops, SparseCore 0:
  9.7 24.5 all-gather.2
  144.4 380.0 all-reduce.7
  528.5 187.8 all-gather.4
  721.7 145.9 all-reduce.11
  870.3 44.3 all-reduce.9
where the time goes:
time: 934 us; the launch traced here: 926 us
  waiting for transfers between devices  467 us (50%)
  blocking collectives  202 us (22%)
  matrix products  144 us (15%)
  local copies, waits for them, and re-layouts  87.7 us (9%)
  between operations  16.4 us (2%)
    unnamed x7, waiting for transfers between devices  257 us
    all_gather x1, waiting for transfers between devices, body(): lax.all_gather(outgoing.reshape(own_count, tile_side, feature_width), 'co...  185 us
    unnamed x1, blocking collectives  135 us
    psum x1, blocking collectives, body(): lax.psum((jnp.dot(node_features.T, grad_pre, precision=HIGHEST), jnp.dot(...  67.3 us
    unnamed x30, local copies, waits for them, and re-layouts  58 us
    dot_general x1, matrix products, tile_products(): return jnp.einsum('tij,tjf->tif', values, picked, precision=HIGHEST)  49.1 us
    dot_general x1, matrix products, tile_backs(): return jnp.einsum('tij,tif->tjf', values, picked, precision=HIGHEST)  49 us
    all_gather x1, waiting for transfers between devices, body(): slab = lax.all_gather(own_blocks, 'row', axis=0, tiled=True)  24.9 us
  transfers between devices with their start and end apart: 5, of which 4 were waited for; matrix products, arithmetic and copies ran while one was open for 13% of the time, Pallas kernels for 0%

commit v1 on v0

v1 whole, which is shorter than its diff:
```python
import functools

import jax
import jax.numpy as jnp
from jax import lax
from jax.experimental import pallas as pl
from jax.experimental.pallas import tpu as pltpu
from jax.sharding import PartitionSpec as P

EPSILON = 1e-05
F32 = jnp.float32
BF16 = jnp.bfloat16
MESH = pl.DeviceIdType.MESH
TILE = 128
WIDTH = 256
SLOTS = 192
DESTS = 64
SOURCES = 8
ROWS = 264
CHUNK = 16
CHUNKS = SLOTS // CHUNK
UNROLL = 4
RING = 16
LAG = 2
VMEM_LIMIT = 60 * 1024 * 1024

VM = pl.BlockSpec(memory_space=pltpu.VMEM)
SM = pl.BlockSpec(memory_space=pltpu.SMEM)
ANY = pl.BlockSpec(memory_space=pl.ANY)
DMA = pltpu.SemaphoreType.DMA


def split(a):
    hi = a.astype(BF16)
    return hi, (a - hi.astype(F32)).astype(BF16)


def mm(a, b, dims=((1,), (0,))):
    return lax.dot_general(a, b, (dims, ((), ())), preferred_element_type=F32)


def dot3(a, b, dims=((1,), (0,))):
    ah, al = split(a)
    bh, bl = split(b)
    return mm(ah, bh, dims) + (mm(ah, bl, dims) + mm(al, bh, dims))


def enter(devices):
    barrier = pltpu.get_barrier_semaphore()
    for device in devices:
        pl.semaphore_signal(barrier, inc=1, device_id=device, device_id_type=MESH)
    pl.semaphore_wait(barrier, len(devices))


def remote(src, dst, send, recv, device):
    return pltpu.make_async_remote_copy(
        src_ref=src, dst_ref=dst, send_sem=send, recv_sem=recv, device_id=device, device_id_type=MESH
    )


def gather_kernel(x_ref, out_ref, local_sem, send, recv):
    row, col = lax.axis_index("row"), lax.axis_index("col")
    hi, core = lax.div(row, 2), lax.rem(row, 2)
    mate = hi * 2 + (1 - core)
    far = (1 - hi) * 2 + core
    far_mate = (1 - hi) * 2 + (1 - core)
    enter([(mate, col), (far, col)])
    n = x_ref.shape[0]
    at = lambda r: out_ref.at[pl.ds(pl.multiple_of(r * n, n), n)]
    own = pltpu.make_async_copy(x_ref, at(row), local_sem)
    own.start()
    across = remote(x_ref, at(row), send.at[0], recv.at[0], (far, col))
    across.start()
    beside = remote(x_ref, at(row), send.at[1], recv.at[1], (mate, col))
    beside.start()
    across.wait_recv()
    onward = remote(at(far), at(far), send.at[2], recv.at[2], (mate, col))
    onward.start()
    beside.wait_recv()
    onward.wait_recv()
    own.wait()
    across.wait_send()
    beside.wait_send()
    onward.wait_send()


def gather_rows(x):
    return pl.pallas_call(
        gather_kernel,
        out_shape=jax.ShapeDtypeStruct((4 * x.shape[0], x.shape[1]), F32),
        in_specs=[VM],
        out_specs=VM,
        scratch_shapes=[DMA, DMA((3,)), DMA((3,))],
        compiler_params=pltpu.CompilerParams(collective_id=0, has_side_effects=True),
        name="gather_rows",
    )(x)


def tile_copy(tiles_hbm, tiles, sems, c):
    at = pl.ds(c * CHUNK, CHUNK)
    return pltpu.make_async_copy(tiles_hbm.at[at], tiles.at[at], sems.at[c])


def forward_kernel(dest, source, count, x_ref, tiles_hbm, out_hbm, tiles, acc, total, xhh, xlo, sems, out_sem):
    for c in range(CHUNKS):
        tile_copy(tiles_hbm, tiles, sems, c).start()
    live = count[0]
    for s in range(SOURCES):
        hi, lo = split(x_ref[s * TILE : (s + 1) * TILE, :])
        xhh[s, 0:TILE, :] = hi
        xhh[s, TILE:, :] = hi
        xlo[s] = lo

    def clear(d, _):
        acc[d] = jnp.zeros((ROWS, TILE), F32)
        total[d] = jnp.zeros((TILE, TILE), F32)
        return 0

    lax.fori_loop(0, DESTS + 1, clear, 0)

    def one(t):
        s = source[t]
        d = jnp.where(t < live, dest[t], DESTS)
        a = tiles[t]
        hi, lo = split(a)
        p = mm(jnp.concatenate([hi, lo], axis=1), xhh[s]) + mm(hi, xlo[s])
        acc[d, 0:TILE, :] += p[:, 0:TILE]
        acc[d, TILE : 2 * TILE, :] += p[:, TILE:]
        total[d] += a

    def group(g, _):
        for u in range(UNROLL):
            one(g * UNROLL + u)
        return 0

    def chunk(c, _):
        tile_copy(tiles_hbm, tiles, sems, c).wait()
        per = CHUNK // UNROLL
        return lax.fori_loop(c * per, (c + 1) * per, group, 0)

    lax.fori_loop(0, CHUNKS, chunk, 0)
    ones = jnp.ones((8, 2 * TILE), BF16)

    def degrees(g, _):
        for u in range(4):
            d = g * 4 + u
            hi, lo = split(total[d])
            acc[d, 2 * TILE :, :] = mm(ones, jnp.concatenate([hi, lo], axis=1), ((1,), (1,)))
        return 0

    lax.fori_loop(0, DESTS // 4, degrees, 0)
    out = pltpu.make_async_copy(acc.at[pl.ds(0, DESTS)], out_hbm, out_sem)
    out.start()
    out.wait()


def forward_tiles(dest, source, count, slab, values):
    return pl.pallas_call(
        forward_kernel,
        out_shape=jax.ShapeDtypeStruct((DESTS, ROWS, TILE), F32),
        in_specs=[SM, SM, SM, VM, ANY],
        out_specs=ANY,
        scratch_shapes=[
            pltpu.VMEM((SLOTS, TILE, TILE), F32),
            pltpu.VMEM((DESTS + 1, ROWS, TILE), F32),
            pltpu.VMEM((DESTS + 1, TILE, TILE), F32),
            pltpu.VMEM((SOURCES, 2 * TILE, WIDTH), BF16),
            pltpu.VMEM((SOURCES, TILE, WIDTH), BF16),
            DMA((CHUNKS,)),
            DMA,
        ],
        compiler_params=pltpu.CompilerParams(vmem_limit_bytes=VMEM_LIMIT),
        cost_estimate=pl.CostEstimate(
            flops=SLOTS * 6 * TILE * TILE * WIDTH, bytes_accessed=22_000_000, transcendentals=0
        ),
        name="forward_tiles",
    )(dest, source, count, slab, values)


def place(cycle, x, y):
    return (4 * x if cycle == 0 else 4 * y) + lax.rem(x + y, 4)


def chip(cycle, q):
    a = lax.div(q, 4)
    b = lax.rem(lax.rem(q, 4) + 4 - a, 4)
    return (a, b) if cycle == 0 else (b, a)


def step_place(p, k, t):
    return lax.rem(p + RING - t, RING) if k % 2 == 0 else lax.rem(p + t, RING)


SUM_ROWS = {(0, 0): (0, 136), (1, 0): (136, 128), (0, 1): (0, 128), (1, 1): (128, 136)}


def rms_silu(pre, cot):
    sig = 1.0 / (1.0 + jnp.exp(-pre))
    s = pre * sig
    r = lax.rsqrt(jnp.mean(s * s, axis=-1, keepdims=True) + EPSILON)
    inner = jnp.mean(cot * s, axis=-1, keepdims=True)
    ds = r * cot - s * (r * r * r * inner)
    return s * r, ds * sig * (1.0 + pre * (1.0 - sig))


PARTS = 32
PART_ROWS = 40
AR_SENDS = 17


def exchange_kernel(
    part_hbm, x_ref, ws_ref, wn_ref, bias_ref, cot_ref,
    layer_out, direct_out, g_out, gw_out,
    acc, rbuf, zbuf, gath, gwp, gws, r1, r2, r3, r4, own_part,
    load_sem, rs_send, rs_recv, zs_send, zs_recv, ag_send, ag_recv, zg_send, zg_recv, ar_send, ar_recv, out_sem,
):
    row, col = lax.axis_index("row"), lax.axis_index("col")
    zh, core = lax.div(row, 2), lax.rem(row, 2)
    x, y, z = lax.div(col, 8), lax.rem(lax.div(col, 2), 4), lax.rem(col, 2)
    column = lambda xx, yy, zz: xx * 8 + yy * 2 + zz
    places = [place(0, x, y), place(1, x, y)]
    nexts = []
    for k in range(4):
        q = lax.rem(places[k // 2] + (1 if k % 2 == 0 else RING - 1), RING)
        nexts.append((row, column(*chip(k // 2, q), z)))
    z_mate = (row, column(x, y, 1 - z))
    core_mate = (zh * 2 + (1 - core), col)
    x_others = [(row, column(lax.rem(x + d, 4), y, z)) for d in range(1, 4)]
    y_others = [(row, column(x, lax.rem(y + d, 4), z)) for d in range(1, 4)]
    far = (1 - zh) * 2 + core
    z_others = [z_mate, (far, col), (far, column(x, y, 1 - z))]

    def block(k, t, zz):
        bx, by = chip(k // 2, step_place(places[k // 2], k, t))
        return (bx * 4 + by) * 4 + zz * 2 + k % 2

    def load(k, sub, t):
        at = (block(k, t + 1, z if sub == 0 else 1 - z), pl.ds(*SUM_ROWS[k // 2, sub]))
        return pltpu.make_async_copy(part_hbm.at[at], acc.at[at], load_sem.at[k, sub, t])

    for k in range(4):
        for sub in (1, 0):
            load(k, sub, 0).start()
            load(k, sub, 1).start()
    enter([core_mate] + x_others + y_others + z_others)

    def sum_send(k, sub, t):
        at = (block(k, t + 1, z if sub == 0 else 1 - z), pl.ds(*SUM_ROWS[k // 2, sub]))
        to = rbuf.at[k, sub, t, pl.ds(0, SUM_ROWS[k // 2, sub][1])]
        return remote(acc.at[at], to, rs_send.at[k, sub, t], rs_recv.at[k, sub, t], nexts[k])

    def mate_send(k):
        at = pl.ds(*SUM_ROWS[k // 2, 1])
        b = block(k, 0, 1 - z)
        return remote(acc.at[b, at], zbuf.at[k % 2, at], zs_send.at[k], zs_recv.at[k], z_mate)

    def add_arrived(k, sub, t):
        sum_send(k, sub, t - 1).wait_recv()
        first, n = SUM_ROWS[k // 2, sub]
        b = block(k, t + 1, z if sub == 0 else 1 - z)
        acc[b, first : first + n, :] += rbuf[k, sub, t - 1, 0:n, :]

    def sum_step(sub, t):
        for k in range(4):

            @pl.when(t + 2 <= RING - 1)
            def _():
                load(k, sub, t + 2).start()

            load(k, sub, t).wait()

            @pl.when(t >= 1)
            def _():
                add_arrived(k, sub, t)

            @pl.when(t <= RING - 2)
            def _():
                sum_send(k, sub, t).start()

            if sub == 1:

                @pl.when(t == RING - 1)
                def _():
                    mate_send(k).start()

    def sum_loop(i, _):
        @pl.when(i <= RING - 1)
        def _():
            sum_step(1, i)

        @pl.when(i >= LAG)
        def _():
            sum_step(0, i - LAG)

        return 0

    lax.fori_loop(0, RING + LAG, sum_loop, 0)

    own = (x * 4 + y) * 4 + z * 2
    x_own = x_ref[...]
    ws, wn = ws_ref[...], wn_ref[...]
    own_term = dot3(x_own, ws)
    for k in range(4):
        mate_send(k).wait_recv()
    sums, inv = [], []
    for h in range(2):
        s = acc[own + h] + zbuf[h]
        degree = jnp.transpose(jnp.broadcast_to(s[2 * TILE : 2 * TILE + 1, :], (TILE, TILE)))
        root = lax.rsqrt(1.0 + degree)
        inv.append(jnp.concatenate([root, root], axis=1))
        sums.append(jnp.concatenate([s[0:TILE], s[TILE : 2 * TILE]], axis=1))
    inv = jnp.concatenate(inv, axis=0)
    neighbour = jnp.concatenate(sums, axis=0) * inv
    pre = own_term + dot3(neighbour, wn) + bias_ref[...]
    out, grad_pre = rms_silu(pre, cot_ref[...])
    layer_out[...] = out
    spread = dot3(grad_pre, wn, ((1,), (1,))) * inv
    for h in range(2):
        for half in range(2):
            gath[own + h, half * TILE : (half + 1) * TILE, :] = spread[
                h * TILE : (h + 1) * TILE, half * TILE : (half + 1) * TILE
            ]

    def rows_of(k):
        return pl.ds((k // 2) * TILE, TILE)

    def mate_give(k):
        at = (own + k % 2, rows_of(k))
        return remote(gath.at[at], gath.at[at], zg_send.at[k], zg_recv.at[k], z_mate)

    def mate_take(k):
        at = (block(k, 0, 1 - z), rows_of(k))
        return remote(gath.at[at], gath.at[at], zg_send.at[k], zg_recv.at[k], z_mate)

    def pass_on(k, sub, t):
        at = (block(k, t, z if sub == 0 else 1 - z), rows_of(k))
        return remote(gath.at[at], gath.at[at], ag_send.at[k, sub, t], ag_recv.at[k, sub, t], nexts[k])

    def take(k, sub, t):
        at = (block(k, t + 1, z if sub == 0 else 1 - z), rows_of(k))
        return remote(gath.at[at], gath.at[at], ag_send.at[k, sub, t], ag_recv.at[k, sub, t], nexts[k])

    for k in range(4):
        mate_give(k).start()
    for k in range(4):
        pass_on(k, 0, 0).start()

    gs = dot3(x_own, grad_pre, ((0,), (0,)))
    gn = dot3(neighbour, grad_pre, ((0,), (0,)))
    flat = [gs[:, 0:TILE], gs[:, TILE:], gn[:, 0:TILE], gn[:, TILE:]]
    gb = jnp.sum(grad_pre, axis=0, keepdims=True)
    gwp[...] = jnp.zeros_like(gwp)
    for i, f in enumerate(flat):
        gwp[i * WIDTH : (i + 1) * WIDTH, :] = f
    gwp[4 * WIDTH : 4 * WIDTH + 1, :] = gb[:, 0:TILE]
    gwp[4 * WIDTH + 1 : 4 * WIDTH + 2, :] = gb[:, TILE:]
    direct_out[...] = dot3(grad_pre, ws, ((1,), (1,)))

    n_core, n_x, n_y = 16 * PART_ROWS, 4 * PART_ROWS, PART_ROWS
    rows_at = lambda c, xx, yy, n: pl.ds(pl.multiple_of((c * 16 + xx * 4 + yy) * PART_ROWS, 8), n)
    span = lambda *at: gwp.at[rows_at(*at)]
    summed = lambda *at: gws.at[rows_at(*at)]
    hop = lambda i, src, dst, device: remote(src, dst, ar_send.at[i], ar_recv.at[i], device)
    zi = zh * 2 + z

    c1 = [hop(0, span(1 - core, 0, 0, n_core), r1, core_mate)]
    c2 = [hop(d, span(core, lax.rem(x + d, 4), 0, n_x), r2.at[d - 1], x_others[d - 1]) for d in range(1, 4)]
    c3 = [hop(3 + d, span(core, x, lax.rem(y + d, 4), n_y), r3.at[d - 1], y_others[d - 1]) for d in range(1, 4)]
    c4 = [hop(7 + d, own_part, r4.at[d], z_others[d]) for d in range(3)]
    mine = summed(core, x, y, n_y)
    c5 = [hop(9 + d, mine, mine, y_others[d - 1]) for d in range(1, 4)]
    mine_x = summed(core, x, 0, n_x)
    c6 = [hop(12 + d, mine_x, mine_x, x_others[d - 1]) for d in range(1, 4)]
    mine_c = summed(core, 0, 0, n_core)
    c7 = [hop(16, mine_c, mine_c, core_mate)]

    def launch(copies):
        for c in copies:
            c.start()

    def land(copies):
        for c in copies:
            c.wait()

    def add_parts(n, c, xx, terms):
        at = pl.ds(pl.multiple_of((core * 16 + c) * PART_ROWS, 8), n)
        v = gwp[at, :]
        for term in terms:
            v = v + term
        gwp[at, :] = v

    def phase0():
        launch(c1)

    def phase1():
        land(c1)
        add_parts(n_core, 0, 0, [r1[...]])
        launch(c2)

    def phase2():
        land(c2)
        add_parts(n_x, x * 4, 0, [r2[d] for d in range(3)])
        launch(c3)

    def phase3():
        land(c3)
        at = pl.ds(pl.multiple_of((core * 16 + x * 4 + y) * PART_ROWS, 8), n_y)
        own_part[...] = gwp[at, :] + r3[0] + r3[1] + r3[2]
        launch(c4)

    def phase4():
        land(c4)
        at = pl.ds(pl.multiple_of((core * 16 + x * 4 + y) * PART_ROWS, 8), n_y)
        gws[at, :] = (own_part[...] + r4[0]) + (r4[1] + r4[2])
        launch(c5)

    def phase5():
        for d in range(1, 4):
            peer = summed(core, x, lax.rem(y + 4 - d, 4), n_y)
            hop(9 + d, peer, peer, y_others[d - 1]).wait_recv()
        for c in c5:
            c.wait_send()
        launch(c6)

    def phase6():
        for d in range(1, 4):
            peer = summed(core, lax.rem(x + 4 - d, 4), 0, n_x)
            hop(12 + d, peer, peer, x_others[d - 1]).wait_recv()
        launch(c7)

    def phase7():
        peer = summed(1 - core, 0, 0, n_core)
        hop(16, peer, peer, core_mate).wait_recv()

    phases = [phase0, phase1, phase2, phase3, phase4, phase5, phase6, phase7]
    del zi

    def gather_step(sub, t):
        for k in range(4):
            if sub == 0:
                take(k, 0, t - 1).wait_recv()
            else:

                @pl.when(t == 0)
                def _():
                    mate_take(k).wait_recv()

                @pl.when(t >= 1)
                def _():
                    take(k, 1, t - 1).wait_recv()

            @pl.when(t <= RING - 2)
            def _():
                pass_on(k, sub, t).start()

    phase0()

    def gather_loop(i, _):
        @pl.when(i <= RING - 1)
        def _():
            gather_step(0, i)

        @pl.when(i >= LAG)
        def _():
            gather_step(1, i - LAG)

        for n in range(1, 8):

            @pl.when(i == 2 * n + 1)
            def _():
                phases[n]()

        return 0

    lax.fori_loop(1, RING + LAG, gather_loop, 0)
    out = pltpu.make_async_copy(gath, g_out, out_sem)
    out.start()
    gw_out[...] = gws[0 : 4 * WIDTH + 8, :]

    def drain(t, _):
        for k in range(4):
            for sub in range(2):
                sum_send(k, sub, t).wait_send()
                pass_on(k, sub, t).wait_send()
        return 0

    lax.fori_loop(0, RING - 1, drain, 0)
    for k in range(4):
        mate_send(k).wait_send()
        mate_give(k).wait_send()
    for copies in (c6, c7):
        for c in copies:
            c.wait_send()
    out.wait()


def exchange(part, x, ws, wn, bias, cot):
    n = x.shape[0]
    steps = RING - 1
    return pl.pallas_call(
        exchange_kernel,
        out_shape=(
            jax.ShapeDtypeStruct((n, WIDTH), F32),
            jax.ShapeDtypeStruct((n, WIDTH), F32),
            jax.ShapeDtypeStruct((DESTS, 2 * TILE, TILE), F32),
            jax.ShapeDtypeStruct((4 * WIDTH + 8, TILE), F32),
        ),
        in_specs=[ANY, VM, VM, VM, VM, VM],
        out_specs=(VM, VM, ANY, VM),
        scratch_shapes=[
            pltpu.VMEM((DESTS, ROWS, TILE), F32),
            pltpu.VMEM((4, 2, steps, 136, TILE), F32),
            pltpu.VMEM((2, ROWS, TILE), F32),
            pltpu.VMEM((DESTS, 2 * TILE, TILE), F32),
            pltpu.VMEM((PARTS * PART_ROWS, TILE), F32),
            pltpu.VMEM((PARTS * PART_ROWS, TILE), F32),
            pltpu.VMEM((16 * PART_ROWS, TILE), F32),
            pltpu.VMEM((3, 4 * PART_ROWS, TILE), F32),
            pltpu.VMEM((3, PART_ROWS, TILE), F32),
            pltpu.VMEM((3, PART_ROWS, TILE), F32),
            pltpu.VMEM((PART_ROWS, TILE), F32),
            DMA((4, 2, RING)),
            DMA((4, 2, steps)),
            DMA((4, 2, steps)),
            DMA((4,)),
            DMA((4,)),
            DMA((4, 2, steps)),
            DMA((4, 2, steps)),
            DMA((4,)),
            DMA((4,)),
            DMA((AR_SENDS,)),
            DMA((AR_SENDS,)),
            DMA,
        ],
        compiler_params=pltpu.CompilerParams(
            collective_id=1, has_side_effects=True, vmem_limit_bytes=VMEM_LIMIT
        ),
        name="exchange",
    )(part, x, ws, wn, bias.reshape(1, WIDTH), cot)


def backward_kernel(dest, source, count, g_hbm, tiles_hbm, out_ref, tiles, g, ghh, glo, acc, sems, g_sem):
    g_copy = pltpu.make_async_copy(g_hbm, g, g_sem)
    g_copy.start()
    for c in range(CHUNKS):
        tile_copy(tiles_hbm, tiles, sems, c).start()
    live = count[0]

    def clear(s, _):
        acc[s] = jnp.zeros((TILE, WIDTH), F32)
        return 0

    lax.fori_loop(0, SOURCES + 1, clear, 0)
    g_copy.wait()

    def cut(d, _):
        for half in range(2):
            hi, lo = split(g[d, half * TILE : (half + 1) * TILE, :])
            lanes = slice(half * TILE, (half + 1) * TILE)
            ghh[d, 0:TILE, lanes] = hi
            ghh[d, TILE:, lanes] = hi
            glo[d, :, lanes] = lo
        return 0

    lax.fori_loop(0, DESTS, cut, 0)

    def one(t):
        d = dest[t]
        s = jnp.where(t < live, source[t], SOURCES)
        hi, lo = split(tiles[t])
        p = mm(jnp.concatenate([hi, lo], axis=0), ghh[d], ((0,), (0,))) + mm(hi, glo[d], ((0,), (0,)))
        acc[s] += p

    def group(g_, _):
        for u in range(UNROLL):
            one(g_ * UNROLL + u)
        return 0

    def chunk(c, _):
        tile_copy(tiles_hbm, tiles, sems, c).wait()
        per = CHUNK // UNROLL
        return lax.fori_loop(c * per, (c + 1) * per, group, 0)

    lax.fori_loop(0, CHUNKS, chunk, 0)
    for s in range(SOURCES):
        out_ref[s * TILE : (s + 1) * TILE, :] = acc[s]


def backward_tiles(dest, source, count, g, values):
    return pl.pallas_call(
        backward_kernel,
        out_shape=jax.ShapeDtypeStruct((SOURCES * TILE, WIDTH), F32),
        in_specs=[SM, SM, SM, ANY, ANY],
        out_specs=VM,
        scratch_shapes=[
            pltpu.VMEM((SLOTS, TILE, TILE), F32),
            pltpu.VMEM((DESTS, 2 * TILE, TILE), F32),
            pltpu.VMEM((DESTS, 2 * TILE, WIDTH), BF16),
            pltpu.VMEM((DESTS, TILE, WIDTH), BF16),
            pltpu.VMEM((SOURCES + 1, TILE, WIDTH), F32),
            DMA((CHUNKS,)),
            DMA,
        ],
        compiler_params=pltpu.CompilerParams(vmem_limit_bytes=VMEM_LIMIT),
        cost_estimate=pl.CostEstimate(
            flops=SLOTS * 6 * TILE * TILE * WIDTH, bytes_accessed=22_000_000, transcendentals=0
        ),
        name="backward_tiles",
    )(dest, source, count, g, values)


def scatter_kernel(back_ref, direct_ref, out_ref, near, cross, send_buf, send, recv):
    row, col = lax.axis_index("row"), lax.axis_index("col")
    hi, core = lax.div(row, 2), lax.rem(row, 2)
    mate = hi * 2 + (1 - core)
    far = (1 - hi) * 2 + core
    far_mate = (1 - hi) * 2 + (1 - core)
    enter([(mate, col), (far, col)])
    n = direct_ref.shape[0]
    at = lambda r: pl.ds(pl.multiple_of(r * n, n), n)
    first = remote(back_ref.at[at(far_mate)], near.at[0], send.at[0], recv.at[0], (mate, col))
    first.start()
    second = remote(back_ref.at[at(mate)], near.at[1], send.at[1], recv.at[1], (mate, col))
    second.start()
    first.wait_recv()
    send_buf[...] = back_ref[at(far), :] + near[0]
    third = remote(send_buf, cross, send.at[2], recv.at[2], (far, col))
    third.start()
    second.wait_recv()
    total = direct_ref[...] + back_ref[at(row), :] + near[1]
    third.wait_recv()
    out_ref[...] = total + cross[...]
    first.wait_send()
    second.wait_send()
    third.wait_send()


def scatter_rows(back, direct):
    n = direct.shape[0]
    return pl.pallas_call(
        scatter_kernel,
        out_shape=jax.ShapeDtypeStruct((n, WIDTH), F32),
        in_specs=[VM, VM],
        out_specs=VM,
        scratch_shapes=[
            pltpu.VMEM((2, n, WIDTH), F32),
            pltpu.VMEM((n, WIDTH), F32),
            pltpu.VMEM((n, WIDTH), F32),
            DMA((3,)),
            DMA((3,)),
        ],
        compiler_params=pltpu.CompilerParams(collective_id=2, has_side_effects=True),
        name="scatter_rows",
    )(back, direct)


def body(x, ws, wn, bias, tile_values, tile_dest, tile_source, tile_count, cot):
    values = tile_values.reshape(SLOTS, TILE, TILE)
    dest, source, count = tile_dest.reshape(SLOTS), tile_source.reshape(SLOTS), tile_count.reshape(1)
    slab = gather_rows(x)
    part = forward_tiles(dest, source, count, slab, values)
    layer_out, direct, g, gw = exchange(part, x, ws, wn, bias, cot)
    back = backward_tiles(dest, source, count, g, values)
    grad_x = scatter_rows(back, direct)
    w = lambda i: jnp.concatenate([gw[i * WIDTH : (i + 1) * WIDTH], gw[(i + 1) * WIDTH : (i + 2) * WIDTH]], axis=1)
    grad_bias = gw[4 * WIDTH : 4 * WIDTH + 2].reshape(WIDTH)
    return layer_out, grad_x, w(0), w(2), grad_bias


def solution(mesh):
    in_specs = (
        P(("col", "row"), None),
        P(),
        P(),
        P(),
        P("row", "col", None, None, None),
        P("row", "col", None),
        P("row", "col", None),
        P("row", "col"),
        P(("col", "row"), None),
    )
    out_specs = (P(("col", "row"), None), P(("col", "row"), None), P(), P(), P())
    return jax.shard_map(body, mesh=mesh, in_specs=in_specs, out_specs=out_specs, check_vma=False)
```

time: 934 us -> 245 us (0.26)
  waiting for transfers between devices: 467 us -> 0 us
  Pallas kernels: 0 us -> 238 us
  blocking collectives: 202 us -> 0 us
  matrix products: 144 us -> 0 us
  local copies, waits for them, and re-layouts: 87.7 us -> 4.75 us
  between operations: 16.4 us -> 1.33 us
    unnamed x7 -> x0, waiting for transfers between devices: 257 us -> none
    pallas_call x0 -> x5, Pallas kernels: none -> 238 us  [the longest x1 151 us: exchange(): pl.pallas_call(exchange_kernel, out_shape=(jax.ShapeDtypeStruct((n, WIDTH...]
    all_gather x2 -> x0, waiting for transfers between devices: 210 us -> none  [the longest x1 185 us: body(): lax.all_gather(outgoing.reshape(own_count, tile_side, feature_width), 'co...]
    dot_general x11 -> x0, matrix products: 144 us -> none  [the longest x1 49.1 us: tile_products(): return jnp.einsum('tij,tjf->tif', values, picked, precision=HIGHEST)]
    unnamed x1 -> x0, blocking collectives: 135 us -> none
    psum x1 -> x0, blocking collectives: 67.3 us -> none  [body(): lax.psum((jnp.dot(node_features.T, grad_pre, precision=HIGHEST), jnp.dot(...]
    unnamed x30 -> x4, local copies, waits for them, and re-layouts: 58 us -> 2.38 us
    gather x2 -> x0, local copies, waits for them, and re-layouts: 29.3 us -> none  [the longest x1 15.8 us: body(): back_terms = tile_backs(values, gathered[dest_ids])]
  transfers between devices with their start and end apart: 5 -> 0, of which waited for: 4 -> 0; matrix products, arithmetic and copies ran while one was open for 13% -> 0% of each run, Pallas kernels for 0% -> 0%
where the time goes in v1:
time: 245 us
  Pallas kernels  238 us (97%)
  local copies, waits for them, and re-layouts  4.75 us (2%)
    pallas_call x1, Pallas kernels, exchange(): pl.pallas_call(exchange_kernel, out_shape=(jax.ShapeDtypeStruct((n, WIDTH...  151 us
    pallas_call x1, Pallas kernels, backward_tiles(): pl.pallas_call(backward_kernel, out_shape=jax.ShapeDtypeStruct((SOURCES *...  27.1 us
    pallas_call x1, Pallas kernels, forward_tiles(): pl.pallas_call(forward_kernel, out_shape=jax.ShapeDtypeStruct((DESTS, ROW...  23.8 us
    pallas_call x1, Pallas kernels, scatter_rows(): pl.pallas_call(scatter_kernel, out_shape=jax.ShapeDtypeStruct((n, WIDTH),...  20.6 us
    pallas_call x1, Pallas kernels, gather_rows(): pl.pallas_call(gather_kernel, out_shape=jax.ShapeDtypeStruct((4 * x.shape...  15.4 us

profile of v1, /device:TPU:1, one launch (start us, length us, event | category | flops | bytes accessed | tf_op | source)
XLA Modules:
  0.0 244.9 jit_solution(2249419448134128759)
XLA Ops:
  1.3 15.4 %gather_rows.1.x_ref = f32[1024,256]{1,0:T(8,128)} custom-call(f32[256,256]{1,0:T(8,128)} %x_ref.3), custom_call_target="tpu_custom_call" | custom-call | tf_op jit(solution)/shard_map/gather_rows/pallas_call | solution.py:88
  16.7 23.8 %forward_tiles.1.part_hbm = f32[64,264,128]{2,1,0:T(8,128)} custom-call(s32[192]{0:T(256)} %bitcast.11, s32[192]{0:T(256)} %bitcast.13, s32[1]{0:T(128)} %bitcast.7.count, f32[1024,256]{1,0:T(8,128)} %gather_rows.1.x_ref, f32[192,128,128]{2,1,0:T(8,128)} %bitcast.9), custom_call_target="tpu_custom_call" | custom-call | flops 4831838208 | bytes 22000000 | tf_op jit(solution)/shard_map/forward_tiles/pallas_call | solution.py:158
  40.6 151.1 %exchange.1 = (f32[256,256]{1,0:T(8,128)}, f32[256,256]{1,0:T(8,128)}, f32[64,256,128]{2,1,0:T(8,128)}, f32[1032,128]{1,0:T(8,128)}) custom-call(f32[64,264,128]{2,1,0:T(8,128)} %forward_tiles.1.part_hbm, f32[256,256]{1,0:T(8,128)} %x_ref.3, f32[256,256]{1,0:T(8,128)} %ws_ref.1, f32[256,256]{1,0:T(8,128)} %wn_ref.1, f32[1,256]{1,0:T(1,128)} %bitcast.15, ...), custom_call_target="tpu_custom_call" | custom-call | tf_op jit(solution)/shard_map/exchange/pallas_call | solution.py:500
  191.7 1.2 slice_bitcast_fusion
  193.0 1.1 fusion
  194.1 0.8 pad_maximum_fusion
  194.9 0.0 copy-start
  194.9 27.1 %backward_tiles.1.back_ref = f32[1024,256]{1,0:T(8,128)} custom-call(s32[192]{0:T(256)} %bitcast.12, s32[192]{0:T(256)} %bitcast.14, s32[1]{0:T(128)} %bitcast.8.count, f32[64,256,128]{2,1,0:T(8,128)} %get-tuple-element.10.g_hbm, f32[192,128,128]{2,1,0:T(8,128)} %bitcast.10), custom_call_target="tpu_custom_call" | custom-call | flops 4831838208 | bytes 22000000 | tf_op jit(solution)/shard_map/backward_tiles/pallas_call | solution.py:590
  222.0 20.6 %scatter_rows.1 = f32[256,256]{1,0:T(8,128)} custom-call(f32[1024,256]{1,0:T(8,128)} %backward_tiles.1.back_ref, f32[256,256]{1,0:T(8,128)} %get-tuple-element.11.direct_ref), custom_call_target="tpu_custom_call" | custom-call | tf_op jit(solution)/shard_map/scatter_rows/pallas_call | solution.py:640
  242.5 0.0 copy-done
  242.6 0.7 copy.17
  243.3 1.7 copy.18
Async XLA Ops:
  194.9 47.6 %copy-start = (f32[256,256]{1,0:T(8,128)S(1)}, f32[256,256]{1,0:T(8,128)}, u32[]{:S(2)}) copy-start(f32[256,256]{1,0:T(8,128)} %get-tuple-element.24) | copy-start | bytes 786436

commit v2 on v1

--- a/solution.py
+++ b/solution.py
@@ -19,9 +19,7 @@
 ROWS = 264
 CHUNK = 16
 CHUNKS = SLOTS // CHUNK
-UNROLL = 4
-RING = 16
-LAG = 2
+UNROLL = 16
 VMEM_LIMIT = 60 * 1024 * 1024
 
 VM = pl.BlockSpec(memory_space=pltpu.VMEM)
@@ -177,23 +175,6 @@
     )(dest, source, count, slab, values)
 
 
-def place(cycle, x, y):
-    return (4 * x if cycle == 0 else 4 * y) + lax.rem(x + y, 4)
-
-
-def chip(cycle, q):
-    a = lax.div(q, 4)
-    b = lax.rem(lax.rem(q, 4) + 4 - a, 4)
-    return (a, b) if cycle == 0 else (b, a)
-
-
-def step_place(p, k, t):
-    return lax.rem(p + RING - t, RING) if k % 2 == 0 else lax.rem(p + t, RING)
-
-
-SUM_ROWS = {(0, 0): (0, 136), (1, 0): (136, 128), (0, 1): (0, 128), (1, 1): (128, 136)}
-
-
 def rms_silu(pre, cot):
     sig = 1.0 / (1.0 + jnp.exp(-pre))
     s = pre * sig
@@ -206,144 +187,252 @@
 PARTS = 32
 PART_ROWS = 40
 AR_SENDS = 17
+FIRST = 64
+SUM_ROWS = (((0, 136), (136, 128)), ((FIRST, 104), (FIRST + 104, 96)))
+GATH_ROWS = (((0, 128), (128, 128)), ((FIRST, 96), (FIRST + 96, 96)))
+SLICES = 20
 
 
 def exchange_kernel(
     part_hbm, x_ref, ws_ref, wn_ref, bias_ref, cot_ref,
     layer_out, direct_out, g_out, gw_out,
-    acc, rbuf, zbuf, gath, gwp, gws, r1, r2, r3, r4, own_part,
+    acc, relays, arrivals, zfirst, zlast, gath, own_term, gwp, gws, r1, r2, r3, r4, own_part,
     load_sem, rs_send, rs_recv, zs_send, zs_recv, ag_send, ag_recv, zg_send, zg_recv, ar_send, ar_recv, out_sem,
 ):
     row, col = lax.axis_index("row"), lax.axis_index("col")
     zh, core = lax.div(row, 2), lax.rem(row, 2)
     x, y, z = lax.div(col, 8), lax.rem(lax.div(col, 2), 4), lax.rem(col, 2)
     column = lambda xx, yy, zz: xx * 8 + yy * 2 + zz
-    places = [place(0, x, y), place(1, x, y)]
-    nexts = []
-    for k in range(4):
-        q = lax.rem(places[k // 2] + (1 if k % 2 == 0 else RING - 1), RING)
-        nexts.append((row, column(*chip(k // 2, q), z)))
+    ahead = lambda p, d: lax.rem(p + d, 4)
+    x_others = [(row, column(ahead(x, d), y, z)) for d in range(1, 4)]
+    y_others = [(row, column(x, ahead(y, d), z)) for d in range(1, 4)]
     z_mate = (row, column(x, y, 1 - z))
     core_mate = (zh * 2 + (1 - core), col)
-    x_others = [(row, column(lax.rem(x + d, 4), y, z)) for d in range(1, 4)]
-    y_others = [(row, column(x, lax.rem(y + d, 4), z)) for d in range(1, 4)]
     far = (1 - zh) * 2 + core
     z_others = [z_mate, (far, col), (far, column(x, y, 1 - z))]
-
-    def block(k, t, zz):
-        bx, by = chip(k // 2, step_place(places[k // 2], k, t))
-        return (bx * 4 + by) * 4 + zz * 2 + k % 2
-
-    def load(k, sub, t):
-        at = (block(k, t + 1, z if sub == 0 else 1 - z), pl.ds(*SUM_ROWS[k // 2, sub]))
-        return pltpu.make_async_copy(part_hbm.at[at], acc.at[at], load_sem.at[k, sub, t])
-
-    for k in range(4):
-        for sub in (1, 0):
-            load(k, sub, 0).start()
-            load(k, sub, 1).start()
+    zs = (z, 1 - z)
+
+    def index(order, wide, narrow, mine):
+        xx, yy = (wide, narrow) if order == 0 else (narrow, wide)
+        return (xx, yy, zs[mine], order)
+
+    def at_place(order, w, which, mine, j):
+        p, q = (x, y) if order == 0 else (y, x)
+        return index(order, ahead(p, j), ahead(q, which), mine) if w == 0 else index(order, p, ahead(q, j), mine)
+
+    def ring(order, w):
+        others = x_others if order == w else y_others
+        return others[0], others[2]
+
+    def number(order, w, which, mine):
+        return (order * 2 + mine) * 5 + (which if w == 0 else 4)
+
+    class Sum:
+        def __init__(self, order, w, which, mine):
+            self.n = number(order, w, which, mine)
+            self.blk = lambda j: at_place(order, w, which, mine, j % 4)
+            self.top, self.low = SUM_ROWS[mine]
+            up, down = ring(order, w)
+            self.copies = []
+            for i, (j, rows, to, device) in enumerate(
+                (
+                    (2, self.top, relays.at[self.n, 0, pl.ds(0, self.top[1])], up),
+                    (2, self.low, relays.at[self.n, 1, pl.ds(0, self.low[1])], down),
+                    (1, self.low, arrivals.at[self.n, 0, pl.ds(*self.low)], up),
+                    (3, self.top, arrivals.at[self.n, 1, pl.ds(*self.top)], down),
+                    (1, self.top, arrivals.at[self.n, 0, pl.ds(*self.top)], up),
+                    (3, self.low, arrivals.at[self.n, 1, pl.ds(*self.low)], down),
+                )
+            ):
+                src = acc.at[(*self.blk(j), pl.ds(*rows))]
+                self.copies.append(remote(src, to, rs_send.at[self.n, i], rs_recv.at[self.n, i], device))
+
+        def issue(self):
+            for c in self.copies[:4]:
+                c.start()
+
+        def relay(self):
+            for i, (j, rows) in enumerate(((1, self.top), (3, self.low))):
+                self.copies[i].wait_recv()
+                at = (*self.blk(j), pl.ds(*rows), slice(None))
+                acc[at] += relays[self.n, i, 0 : rows[1], :]
+                self.copies[4 + i].start()
+
+        def finish(self):
+            for c in self.copies[2:]:
+                c.wait_recv()
+            rows = pl.ds(self.top[0], self.top[1] + self.low[1])
+            at = (*self.blk(0), rows, slice(None))
+            acc[at] += arrivals[self.n, 0, rows, :] + arrivals[self.n, 1, rows, :]
+
+        def drain(self):
+            for c in self.copies:
+                c.wait_send()
+
+    class Gather:
+        def __init__(self, order, w, which, mine):
+            n = number(order, w, which, mine)
+            blk = lambda j: at_place(order, w, which, mine, j % 4)
+            top, low = GATH_ROWS[mine]
+            up, down = ring(order, w)
+            self.out, self.come = [], []
+            for i, (leaves, comes, rows, device) in enumerate(
+                (
+                    (0, 3, top, up),
+                    (0, 1, low, down),
+                    (0, 3, low, up),
+                    (0, 1, top, down),
+                    (3, 2, top, up),
+                    (1, 2, low, down),
+                )
+            ):
+                for j, kept in ((leaves, self.out), (comes, self.come)):
+                    ref = gath.at[(*blk(j), pl.ds(*rows))]
+                    kept.append(remote(ref, ref, ag_send.at[n, i], ag_recv.at[n, i], device))
+
+        def issue(self):
+            for c in self.out[:4]:
+                c.start()
+
+        def relay(self):
+            for i in range(2):
+                self.come[i].wait_recv()
+                self.out[4 + i].start()
+
+        def near(self):
+            for c in self.come[2:4]:
+                c.wait_recv()
+
+        def finish(self):
+            for c in self.come[4:]:
+                c.wait_recv()
+
+        def drain(self):
+            for c in self.out:
+                c.wait_send()
+
+    def strip(ref, order, which, mine, rows=None):
+        q = ahead(y if order == 0 else x, which)
+        lead = (slice(None), q) if order == 0 else (q, slice(None))
+        return ref.at[(*lead, zs[mine], order) + (() if rows is None else (pl.ds(*rows),))]
+
+    def load(order, which, mine):
+        n = order * 8 + mine * 4 + which
+        return pltpu.make_async_copy(strip(part_hbm, order, which, mine), strip(acc, order, which, mine), load_sem.at[n])
+
+    def z_first(order, which):
+        to = zfirst.at[order, which]
+        i = order * 4 + which
+        return remote(strip(part_hbm, order, which, 1, (0, FIRST)), to, zs_send.at[i], zs_recv.at[i], z_mate)
+
+    def z_last(order):
+        rows = pl.ds(FIRST, ROWS - FIRST)
+        src = acc.at[(*at_place(order, 0, 0, 1, 0), rows)]
+        return remote(src, zlast.at[order, rows], zs_send.at[8 + order], zs_recv.at[8 + order], z_mate)
+
+    turn = [(which, 1) for which in (2, 1, 3, 0)] + [(which, 0) for which in (2, 1, 3, 0)]
+    for which, mine in turn:
+        for order in range(2):
+            load(order, which, mine).start()
     enter([core_mate] + x_others + y_others + z_others)
-
-    def sum_send(k, sub, t):
-        at = (block(k, t + 1, z if sub == 0 else 1 - z), pl.ds(*SUM_ROWS[k // 2, sub]))
-        to = rbuf.at[k, sub, t, pl.ds(0, SUM_ROWS[k // 2, sub][1])]
-        return remote(acc.at[at], to, rs_send.at[k, sub, t], rs_recv.at[k, sub, t], nexts[k])
-
-    def mate_send(k):
-        at = pl.ds(*SUM_ROWS[k // 2, 1])
-        b = block(k, 0, 1 - z)
-        return remote(acc.at[b, at], zbuf.at[k % 2, at], zs_send.at[k], zs_recv.at[k], z_mate)
-
-    def add_arrived(k, sub, t):
-        sum_send(k, sub, t - 1).wait_recv()
-        first, n = SUM_ROWS[k // 2, sub]
-        b = block(k, t + 1, z if sub == 0 else 1 - z)
-        acc[b, first : first + n, :] += rbuf[k, sub, t - 1, 0:n, :]
-
-    def sum_step(sub, t):
-        for k in range(4):
-
-            @pl.when(t + 2 <= RING - 1)
-            def _():
-                load(k, sub, t + 2).start()
-
-            load(k, sub, t).wait()
-
-            @pl.when(t >= 1)
-            def _():
-                add_arrived(k, sub, t)
-
-            @pl.when(t <= RING - 2)
-            def _():
-                sum_send(k, sub, t).start()
-
-            if sub == 1:
-
-                @pl.when(t == RING - 1)
-                def _():
-                    mate_send(k).start()
-
-    def sum_loop(i, _):
-        @pl.when(i <= RING - 1)
-        def _():
-            sum_step(1, i)
-
-        @pl.when(i >= LAG)
-        def _():
-            sum_step(0, i - LAG)
-
-        return 0
-
-    lax.fori_loop(0, RING + LAG, sum_loop, 0)
-
-    own = (x * 4 + y) * 4 + z * 2
+    for which in (2, 1, 3, 0):
+        for order in range(2):
+            z_first(order, which).start()
+
+    wide = [[Sum(order, 0, which, mine) for order in range(2)] for which, mine in turn]
+    narrow = [[Sum(order, 1, 0, mine) for order in range(2)] for mine in range(2)]
+
+    def each(pair, action):
+        for s in pair:
+            getattr(s, action)()
+
+    def sum_issue(i):
+        which, mine = turn[i]
+        for order in range(2):
+            load(order, which, mine).wait()
+            if mine == 0:
+                z_first(order, which).wait_recv()
+                p = y if order == 0 else x
+                for j in range(4):
+                    at = (*index(order, j, ahead(p, which), 0), pl.ds(0, FIRST), slice(None))
+                    acc[at] += zfirst[order, which, j]
+            wide[i][order].issue()
+
+    for i in range(len(turn) + 3):
+        if i < len(turn):
+            sum_issue(i)
+        if i == 0:
+            own_term[...] = dot3(x_ref[...], ws_ref[...])
+        if 1 <= i <= len(turn):
+            each(wide[i - 1], "relay")
+        if i == 5:
+            each(narrow[1], "relay")
+        if i == 9:
+            each(narrow[0], "relay")
+        if 2 <= i <= len(turn) + 1:
+            each(wide[i - 2], "finish")
+        if i == 4:
+            each(narrow[1], "issue")
+        if i == 8:
+            each(narrow[0], "issue")
+        if i == 6:
+            each(narrow[1], "finish")
+            for order in range(2):
+                z_last(order).start()
+        if i == 10:
+            each(narrow[0], "finish")
+
     x_own = x_ref[...]
     ws, wn = ws_ref[...], wn_ref[...]
-    own_term = dot3(x_own, ws)
-    for k in range(4):
-        mate_send(k).wait_recv()
     sums, inv = [], []
-    for h in range(2):
-        s = acc[own + h] + zbuf[h]
+    for order in range(2):
+        z_last(order).wait_recv()
+        own = at_place(order, 0, 0, 0, 0)
+        s = jnp.concatenate([acc[(*own, pl.ds(0, FIRST))], acc[(*own, pl.ds(FIRST, ROWS - FIRST))] + zlast[order, FIRST:, :]], axis=0)
         degree = jnp.transpose(jnp.broadcast_to(s[2 * TILE : 2 * TILE + 1, :], (TILE, TILE)))
         root = lax.rsqrt(1.0 + degree)
         inv.append(jnp.concatenate([root, root], axis=1))
         sums.append(jnp.concatenate([s[0:TILE], s[TILE : 2 * TILE]], axis=1))
     inv = jnp.concatenate(inv, axis=0)
     neighbour = jnp.concatenate(sums, axis=0) * inv
-    pre = own_term + dot3(neighbour, wn) + bias_ref[...]
+    pre = own_term[...] + dot3(neighbour, wn) + bias_ref[...]
     out, grad_pre = rms_silu(pre, cot_ref[...])
     layer_out[...] = out
     spread = dot3(grad_pre, wn, ((1,), (1,))) * inv
-    for h in range(2):
+    for order in range(2):
         for half in range(2):
-            gath[own + h, half * TILE : (half + 1) * TILE, :] = spread[
-                h * TILE : (h + 1) * TILE, half * TILE : (half + 1) * TILE
+            gath[(*at_place(order, 0, 0, 0, 0), pl.ds(half * TILE, TILE), slice(None))] = spread[
+                order * TILE : (order + 1) * TILE, half * TILE : (half + 1) * TILE
             ]
 
-    def rows_of(k):
-        return pl.ds((k // 2) * TILE, TILE)
-
-    def mate_give(k):
-        at = (own + k % 2, rows_of(k))
-        return remote(gath.at[at], gath.at[at], zg_send.at[k], zg_recv.at[k], z_mate)
-
-    def mate_take(k):
-        at = (block(k, 0, 1 - z), rows_of(k))
-        return remote(gath.at[at], gath.at[at], zg_send.at[k], zg_recv.at[k], z_mate)
-
-    def pass_on(k, sub, t):
-        at = (block(k, t, z if sub == 0 else 1 - z), rows_of(k))
-        return remote(gath.at[at], gath.at[at], ag_send.at[k, sub, t], ag_recv.at[k, sub, t], nexts[k])
-
-    def take(k, sub, t):
-        at = (block(k, t + 1, z if sub == 0 else 1 - z), rows_of(k))
-        return remote(gath.at[at], gath.at[at], ag_send.at[k, sub, t], ag_recv.at[k, sub, t], nexts[k])
-
-    for k in range(4):
-        mate_give(k).start()
-    for k in range(4):
-        pass_on(k, 0, 0).start()
+    def give(order, mine):
+        ref = gath.at[(*at_place(order, 0, 0, mine, 0), pl.ds(FIRST, 2 * TILE - FIRST))]
+        return remote(ref, ref, zg_send.at[8 + order], zg_recv.at[8 + order], z_mate)
+
+    def z_after(order, which, mine):
+        ref = strip(gath, order, which, mine, (0, FIRST))
+        i = order * 4 + which
+        return remote(ref, ref, zg_send.at[i], zg_recv.at[i], z_mate)
+
+    def write(order, which, mine):
+        n = order * 8 + mine * 4 + which
+        return pltpu.make_async_copy(strip(gath, order, which, mine), strip(g_out, order, which, mine), out_sem.at[n])
+
+    gwide = {(which, mine): [Gather(order, 0, which, mine) for order in range(2)] for which in range(4) for mine in range(2)}
+    gnarrow = [[Gather(order, 1, 0, mine) for order in range(2)] for mine in range(2)]
+
+    def done(which, mine):
+        each(gwide[which, mine], "near")
+        each(gwide[which, mine], "finish")
+        for order in range(2):
+            if mine == 0:
+                z_after(order, which, 0).start()
+                write(order, which, 0).start()
+
+    for order in range(2):
+        give(order, 0).start()
+    each(gnarrow[0], "issue")
+    each(gwide[0, 0], "issue")
 
     gs = dot3(x_own, grad_pre, ((0,), (0,)))
     gn = dot3(neighbour, grad_pre, ((0,), (0,)))
@@ -354,18 +443,16 @@
         gwp[i * WIDTH : (i + 1) * WIDTH, :] = f
     gwp[4 * WIDTH : 4 * WIDTH + 1, :] = gb[:, 0:TILE]
     gwp[4 * WIDTH + 1 : 4 * WIDTH + 2, :] = gb[:, TILE:]
-    direct_out[...] = dot3(grad_pre, ws, ((1,), (1,)))
 
     n_core, n_x, n_y = 16 * PART_ROWS, 4 * PART_ROWS, PART_ROWS
     rows_at = lambda c, xx, yy, n: pl.ds(pl.multiple_of((c * 16 + xx * 4 + yy) * PART_ROWS, 8), n)
     span = lambda *at: gwp.at[rows_at(*at)]
     summed = lambda *at: gws.at[rows_at(*at)]
     hop = lambda i, src, dst, device: remote(src, dst, ar_send.at[i], ar_recv.at[i], device)
-    zi = zh * 2 + z
 
     c1 = [hop(0, span(1 - core, 0, 0, n_core), r1, core_mate)]
-    c2 = [hop(d, span(core, lax.rem(x + d, 4), 0, n_x), r2.at[d - 1], x_others[d - 1]) for d in range(1, 4)]
-    c3 = [hop(3 + d, span(core, x, lax.rem(y + d, 4), n_y), r3.at[d - 1], y_others[d - 1]) for d in range(1, 4)]
+    c2 = [hop(d, span(core, ahead(x, d), 0, n_x), r2.at[d - 1], x_others[d - 1]) for d in range(1, 4)]
+    c3 = [hop(3 + d, span(core, x, ahead(y, d), n_y), r3.at[d - 1], y_others[d - 1]) for d in range(1, 4)]
     c4 = [hop(7 + d, own_part, r4.at[d], z_others[d]) for d in range(3)]
     mine = summed(core, x, y, n_y)
     c5 = [hop(9 + d, mine, mine, y_others[d - 1]) for d in range(1, 4)]
@@ -382,136 +469,137 @@
         for c in copies:
             c.wait()
 
-    def add_parts(n, c, xx, terms):
-        at = pl.ds(pl.multiple_of((core * 16 + c) * PART_ROWS, 8), n)
+    def add_parts(at, terms):
         v = gwp[at, :]
         for term in terms:
             v = v + term
         gwp[at, :] = v
 
-    def phase0():
-        launch(c1)
-
     def phase1():
         land(c1)
-        add_parts(n_core, 0, 0, [r1[...]])
+        add_parts(rows_at(core, 0, 0, n_core), [r1[...]])
         launch(c2)
 
     def phase2():
         land(c2)
-        add_parts(n_x, x * 4, 0, [r2[d] for d in range(3)])
+        add_parts(rows_at(core, x, 0, n_x), [r2[d] for d in range(3)])
         launch(c3)
 
     def phase3():
         land(c3)
-        at = pl.ds(pl.multiple_of((core * 16 + x * 4 + y) * PART_ROWS, 8), n_y)
-        own_part[...] = gwp[at, :] + r3[0] + r3[1] + r3[2]
+        own_part[...] = gwp[rows_at(core, x, y, n_y), :] + r3[0] + r3[1] + r3[2]
         launch(c4)
 
     def phase4():
         land(c4)
-        at = pl.ds(pl.multiple_of((core * 16 + x * 4 + y) * PART_ROWS, 8), n_y)
-        gws[at, :] = (own_part[...] + r4[0]) + (r4[1] + r4[2])
+        gws[rows_at(core, x, y, n_y), :] = (own_part[...] + r4[0]) + (r4[1] + r4[2])
         launch(c5)
 
     def phase5():
         for d in range(1, 4):
-            peer = summed(core, x, lax.rem(y + 4 - d, 4), n_y)
+            peer = summed(core, x, ahead(y, 4 - d), n_y)
             hop(9 + d, peer, peer, y_others[d - 1]).wait_recv()
-        for c in c5:
-            c.wait_send()
         launch(c6)
 
     def phase6():
         for d in range(1, 4):
-            peer = summed(core, lax.rem(x + 4 - d, 4), 0, n_x)
+            peer = summed(core, ahead(x, 4 - d), 0, n_x)
             hop(12 + d, peer, peer, x_others[d - 1]).wait_recv()
         launch(c7)
 
     def phase7():
         peer = summed(1 - core, 0, 0, n_core)
         hop(16, peer, peer, core_mate).wait_recv()
-
-    phases = [phase0, phase1, phase2, phase3, phase4, phase5, phase6, phase7]
-    del zi
-
-    def gather_step(sub, t):
-        for k in range(4):
-            if sub == 0:
-                take(k, 0, t - 1).wait_recv()
-            else:
-
-                @pl.when(t == 0)
-                def _():
-                    mate_take(k).wait_recv()
-
-                @pl.when(t >= 1)
-                def _():
-                    take(k, 1, t - 1).wait_recv()
-
-            @pl.when(t <= RING - 2)
-            def _():
-                pass_on(k, sub, t).start()
-
-    phase0()
-
-    def gather_loop(i, _):
-        @pl.when(i <= RING - 1)
-        def _():
-            gather_step(0, i)
-
-        @pl.when(i >= LAG)
-        def _():
-            gather_step(1, i - LAG)
-
-        for n in range(1, 8):
-
-            @pl.when(i == 2 * n + 1)
-            def _():
-                phases[n]()
-
-        return 0
-
-    lax.fori_loop(1, RING + LAG, gather_loop, 0)
-    out = pltpu.make_async_copy(gath, g_out, out_sem)
-    out.start()
-    gw_out[...] = gws[0 : 4 * WIDTH + 8, :]
-
-    def drain(t, _):
-        for k in range(4):
-            for sub in range(2):
-                sum_send(k, sub, t).wait_send()
-                pass_on(k, sub, t).wait_send()
-        return 0
-
-    lax.fori_loop(0, RING - 1, drain, 0)
-    for k in range(4):
-        mate_send(k).wait_send()
-        mate_give(k).wait_send()
-    for copies in (c6, c7):
+        gw_out[...] = gws[0 : 4 * WIDTH + 8, :]
+
+    launch(c1)
+    direct_out[...] = dot3(grad_pre, ws, ((1,), (1,)))
+
+    each(gnarrow[0], "relay")
+    each(gwide[0, 0], "relay")
+    each(gnarrow[0], "near")
+    each(gwide[1, 0], "issue")
+    phase1()
+    for order in range(2):
+        give(order, 1).wait_recv()
+    each(gnarrow[1], "issue")
+    each(gwide[3, 0], "issue")
+    each(gwide[1, 0], "relay")
+    done(0, 0)
+    phase2()
+    each(gnarrow[1], "relay")
+    each(gnarrow[0], "finish")
+    each(gwide[2, 0], "issue")
+    each(gwide[3, 0], "relay")
+    done(1, 0)
+    phase3()
+    each(gwide[0, 1], "issue")
+    each(gwide[2, 0], "relay")
+    done(3, 0)
+    each(gnarrow[1], "near")
+    phase4()
+    each(gwide[1, 1], "issue")
+    each(gwide[0, 1], "relay")
+    done(2, 0)
+    each(gnarrow[1], "finish")
+    phase5()
+    each(gwide[3, 1], "issue")
+    each(gwide[1, 1], "relay")
+    done(0, 1)
+    phase6()
+    each(gwide[2, 1], "issue")
+    each(gwide[3, 1], "relay")
+    done(1, 1)
+    phase7()
+    each(gwide[2, 1], "relay")
+    done(3, 1)
+    for which in (0, 1, 3):
+        for order in range(2):
+            z_after(order, which, 1).wait_recv()
+            write(order, which, 1).start()
+    done(2, 1)
+    for order in range(2):
+        z_after(order, 2, 1).wait_recv()
+        write(order, 2, 1).start()
+
+    for pair in wide + narrow + list(gwide.values()) + gnarrow:
+        each(pair, "drain")
+    for order in range(2):
+        z_last(order).wait_send()
+        give(order, 0).wait_send()
+        for which in range(4):
+            z_first(order, which).wait_send()
+            z_after(order, which, 0).wait_send()
+    for copies in (c5, c6, c7):
         for c in copies:
             c.wait_send()
-    out.wait()
+    for which in range(4):
+        for order in range(2):
+            for own_z in range(2):
+                write(order, which, own_z).wait()
 
 
 def exchange(part, x, ws, wn, bias, cot):
     n = x.shape[0]
-    steps = RING - 1
-    return pl.pallas_call(
+    layout = (4, 4, 2, 2)
+    out = pl.pallas_call(
         exchange_kernel,
         out_shape=(
             jax.ShapeDtypeStruct((n, WIDTH), F32),
             jax.ShapeDtypeStruct((n, WIDTH), F32),
-            jax.ShapeDtypeStruct((DESTS, 2 * TILE, TILE), F32),
+            jax.ShapeDtypeStruct((*layout, 2 * TILE, TILE), F32),
             jax.ShapeDtypeStruct((4 * WIDTH + 8, TILE), F32),
         ),
         in_specs=[ANY, VM, VM, VM, VM, VM],
         out_specs=(VM, VM, ANY, VM),
         scratch_shapes=[
-            pltpu.VMEM((DESTS, ROWS, TILE), F32),
-            pltpu.VMEM((4, 2, steps, 136, TILE), F32),
+            pltpu.VMEM((*layout, ROWS, TILE), F32),
+            pltpu.VMEM((SLICES, 2, 136, TILE), F32),
+            pltpu.VMEM((SLICES, 2, ROWS, TILE), F32),
+            pltpu.VMEM((2, 4, 4, FIRST, TILE), F32),
             pltpu.VMEM((2, ROWS, TILE), F32),
-            pltpu.VMEM((DESTS, 2 * TILE, TILE), F32),
+            pltpu.VMEM((*layout, 2 * TILE, TILE), F32),
+            pltpu.VMEM((n, WIDTH), F32),
             pltpu.VMEM((PARTS * PART_ROWS, TILE), F32),
             pltpu.VMEM((PARTS * PART_ROWS, TILE), F32),
             pltpu.VMEM((16 * PART_ROWS, TILE), F32),
@@ -519,24 +607,26 @@
             pltpu.VMEM((3, PART_ROWS, TILE), F32),
             pltpu.VMEM((3, PART_ROWS, TILE), F32),
             pltpu.VMEM((PART_ROWS, TILE), F32),
-            DMA((4, 2, RING)),
-            DMA((4, 2, steps)),
-            DMA((4, 2, steps)),
-            DMA((4,)),
-            DMA((4,)),
-            DMA((4, 2, steps)),
-            DMA((4, 2, steps)),
-            DMA((4,)),
-            DMA((4,)),
+            DMA((16,)),
+            DMA((SLICES, 6)),
+            DMA((SLICES, 6)),
+            DMA((10,)),
+            DMA((10,)),
+            DMA((SLICES, 6)),
+            DMA((SLICES, 6)),
+            DMA((10,)),
+            DMA((10,)),
             DMA((AR_SENDS,)),
             DMA((AR_SENDS,)),
-            DMA,
+            DMA((16,)),
         ],
         compiler_params=pltpu.CompilerParams(
             collective_id=1, has_side_effects=True, vmem_limit_bytes=VMEM_LIMIT
         ),
         name="exchange",
-    )(part, x, ws, wn, bias.reshape(1, WIDTH), cot)
+    )(part.reshape(*layout, ROWS, TILE), x, ws, wn, bias.reshape(1, WIDTH), cot)
+    layer_out, direct, g, gw = out
+    return layer_out, direct, g.reshape(DESTS, 2 * TILE, TILE), gw
 
 
 def backward_kernel(dest, source, count, g_hbm, tiles_hbm, out_ref, tiles, g, ghh, glo, acc, sems, g_sem):

time: 245 us -> 180 us (0.73)
  Pallas kernels: 238 us -> 175 us
    pallas_call x1, Pallas kernels: 151 us -> 106 us  [exchange(): pl.pallas_call(exchange_kernel, out_shape=(jax.ShapeDtypeStruct((n, WIDTH...]
    pallas_call x1, Pallas kernels: 27.1 us -> 19.7 us  [backward_tiles(): pl.pallas_call(backward_kernel, out_shape=jax.ShapeDtypeStruct((SOURCES *...]
    pallas_call x1, Pallas kernels: 20.6 us -> 14.5 us  [scatter_rows(): pl.pallas_call(scatter_kernel, out_shape=jax.ShapeDtypeStruct((n, WIDTH),...]
    pallas_call x1, Pallas kernels: 23.8 us -> 19 us  [forward_tiles(): pl.pallas_call(forward_kernel, out_shape=jax.ShapeDtypeStruct((DESTS, ROW...]
where the time goes in v2:
time: 180 us
  Pallas kernels  175 us (97%)
  local copies, waits for them, and re-layouts  2.98 us (2%)
    pallas_call x1, Pallas kernels, exchange(): pl.pallas_call(exchange_kernel, out_shape=(jax.ShapeDtypeStruct((n, WIDTH...  106 us
    pallas_call x1, Pallas kernels, backward_tiles(): pl.pallas_call(backward_kernel, out_shape=jax.ShapeDtypeStruct((SOURCES *...  19.7 us
    pallas_call x1, Pallas kernels, forward_tiles(): pl.pallas_call(forward_kernel, out_shape=jax.ShapeDtypeStruct((DESTS, ROW...  19 us
    pallas_call x1, Pallas kernels, gather_rows(): pl.pallas_call(gather_kernel, out_shape=jax.ShapeDtypeStruct((4 * x.shape...  15.6 us
    pallas_call x1, Pallas kernels, scatter_rows(): pl.pallas_call(scatter_kernel, out_shape=jax.ShapeDtypeStruct((n, WIDTH),...  14.5 us

profile of v2, /device:TPU:1, one launch (start us, length us, event | category | flops | bytes accessed | tf_op | source)
XLA Modules:
  0.0 180.1 jit_solution(16398182603625541241)
XLA Ops:
  1.3 15.6 %gather_rows.1.x_ref = f32[1024,256]{1,0:T(8,128)} custom-call(f32[256,256]{1,0:T(8,128)} %x_ref.3), custom_call_target="tpu_custom_call" | custom-call | tf_op jit(solution)/shard_map/gather_rows/pallas_call | solution.py:86
  16.8 19.0 %forward_tiles.1 = f32[64,264,128]{2,1,0:T(8,128)} custom-call(s32[192]{0:T(256)} %bitcast.15, s32[192]{0:T(256)} %bitcast.17, s32[1]{0:T(128)} %bitcast.9.count, f32[1024,256]{1,0:T(8,128)} %gather_rows.1.x_ref, f32[192,128,128]{2,1,0:T(8,128)} %bitcast.11), custom_call_target="tpu_custom_call" | custom-call | flops 4831838208 | bytes 22000000 | tf_op jit(solution)/shard_map/forward_tiles/pallas_call | solution.py:156
  35.9 106.2 %exchange.1 = (f32[256,256]{1,0:T(8,128)}, f32[256,256]{1,0:T(8,128)}, f32[4,4,2,2,256,128]{5,4,3,2,1,0:T(8,128)}, f32[1032,128]{1,0:T(8,128)}) custom-call(f32[4,4,2,2,264,128]{5,4,3,2,1,0:T(8,128)} %bitcast.13, f32[256,256]{1,0:T(8,128)} %x_ref.3, f32[256,256]{1,0:T(8,128)} %ws_ref.1, f32[256,256]{1,0:T(8,128)} %wn_ref.1, f32[1,256]{1,0:T(1,128)} %bitcast.19, ...), custom_call_target="tpu_custom_call" | custom-call | tf_op jit(solution)/shard_map/exchange/pallas_call | solution.py:585
  142.1 0.0 copy-start
  142.1 0.0 copy-start.1
  142.1 19.7 %backward_tiles.1.back_ref = f32[1024,256]{1,0:T(8,128)} custom-call(s32[192]{0:T(256)} %bitcast.16, s32[192]{0:T(256)} %bitcast.18, s32[1]{0:T(128)} %bitcast.10.count, f32[64,256,128]{2,1,0:T(8,128)} %bitcast.14, f32[192,128,128]{2,1,0:T(8,128)} %bitcast.12), custom_call_target="tpu_custom_call" | custom-call | flops 4831838208 | bytes 22000000 | tf_op jit(solution)/shard_map/backward_tiles/pallas_call | solution.py:680
  161.8 14.5 %scatter_rows.1 = f32[256,256]{1,0:T(8,128)} custom-call(f32[1024,256]{1,0:T(8,128)} %backward_tiles.1.back_ref, f32[256,256]{1,0:T(8,128)} %get-tuple-element.11.direct_ref), custom_call_target="tpu_custom_call" | custom-call | tf_op jit(solution)/shard_map/scatter_rows/pallas_call | solution.py:730
  176.3 0.0 copy-done
  176.3 0.6 slice_bitcast_fusion
  176.9 0.8 pad_maximum_fusion
  177.7 0.0 copy-done.1
  177.7 0.7 copy.17
  178.4 1.7 copy.18
  (1 shorter events, 0.0 us)
Async XLA Ops:
  142.1 34.2 %copy-start = (f32[1032,128]{1,0:T(8,128)S(1)}, f32[1032,128]{1,0:T(8,128)}, u32[]{:S(2)}) copy-start(f32[1032,128]{1,0:T(8,128)} %get-tuple-element.12) | copy-start | bytes 1585156
  142.1 35.6 %copy-start.1 = (f32[256,256]{1,0:T(8,128)S(1)}, f32[256,256]{1,0:T(8,128)}, u32[]{:S(2)}) copy-start(f32[256,256]{1,0:T(8,128)} %get-tuple-element.24) | copy-start | bytes 786436

commit v3 on v2

--- a/solution.py
+++ b/solution.py
@@ -20,6 +20,7 @@
 CHUNK = 16
 CHUNKS = SLOTS // CHUNK
 UNROLL = 16
+PIECES = 4
 VMEM_LIMIT = 60 * 1024 * 1024
 
 VM = pl.BlockSpec(memory_space=pltpu.VMEM)
@@ -61,25 +62,26 @@
     hi, core = lax.div(row, 2), lax.rem(row, 2)
     mate = hi * 2 + (1 - core)
     far = (1 - hi) * 2 + core
-    far_mate = (1 - hi) * 2 + (1 - core)
     enter([(mate, col), (far, col)])
     n = x_ref.shape[0]
-    at = lambda r: out_ref.at[pl.ds(pl.multiple_of(r * n, n), n)]
-    own = pltpu.make_async_copy(x_ref, at(row), local_sem)
+    m = n // PIECES
+    at = lambda r, c: out_ref.at[pl.ds(pl.multiple_of(r * n + c * m, m), m)]
+    piece = lambda c: x_ref.at[pl.ds(c * m, m)]
+    own = pltpu.make_async_copy(x_ref, out_ref.at[pl.ds(pl.multiple_of(row * n, n), n)], local_sem)
+    across = [remote(piece(c), at(row, c), send.at[0, c], recv.at[0, c], (far, col)) for c in range(PIECES)]
+    beside = [remote(piece(c), at(row, c), send.at[1, c], recv.at[1, c], (mate, col)) for c in range(PIECES)]
+    onward = [remote(at(far, c), at(far, c), send.at[2, c], recv.at[2, c], (mate, col)) for c in range(PIECES)]
+    for c in across + beside:
+        c.start()
     own.start()
-    across = remote(x_ref, at(row), send.at[0], recv.at[0], (far, col))
-    across.start()
-    beside = remote(x_ref, at(row), send.at[1], recv.at[1], (mate, col))
-    beside.start()
-    across.wait_recv()
-    onward = remote(at(far), at(far), send.at[2], recv.at[2], (mate, col))
-    onward.start()
-    beside.wait_recv()
-    onward.wait_recv()
+    for c in range(PIECES):
+        across[c].wait_recv()
+        onward[c].start()
+    for c in beside + onward:
+        c.wait_recv()
     own.wait()
-    across.wait_send()
-    beside.wait_send()
-    onward.wait_send()
+    for c in across + beside + onward:
+        c.wait_send()
 
 
 def gather_rows(x):
@@ -88,7 +90,7 @@
         out_shape=jax.ShapeDtypeStruct((4 * x.shape[0], x.shape[1]), F32),
         in_specs=[VM],
         out_specs=VM,
-        scratch_shapes=[DMA, DMA((3,)), DMA((3,))],
+        scratch_shapes=[DMA, DMA((3, PIECES)), DMA((3, PIECES))],
         compiler_params=pltpu.CompilerParams(collective_id=0, has_side_effects=True),
         name="gather_rows",
     )(x)
@@ -99,15 +101,15 @@
     return pltpu.make_async_copy(tiles_hbm.at[at], tiles.at[at], sems.at[c])
 
 
-def forward_kernel(dest, source, count, x_ref, tiles_hbm, out_hbm, tiles, acc, total, xhh, xlo, sems, out_sem):
+def forward_kernel(dest, source, count, x_ref, tiles_hbm, out_hbm, tiles, acc, total, xs, sems, out_sem):
     for c in range(CHUNKS):
         tile_copy(tiles_hbm, tiles, sems, c).start()
     live = count[0]
     for s in range(SOURCES):
         hi, lo = split(x_ref[s * TILE : (s + 1) * TILE, :])
-        xhh[s, 0:TILE, :] = hi
-        xhh[s, TILE:, :] = hi
-        xlo[s] = lo
+        xs[s, 0:TILE, :] = hi
+        xs[s, TILE : 2 * TILE, :] = hi
+        xs[s, 2 * TILE :, :] = lo
 
     def clear(d, _):
         acc[d] = jnp.zeros((ROWS, TILE), F32)
@@ -121,7 +123,7 @@
         d = jnp.where(t < live, dest[t], DESTS)
         a = tiles[t]
         hi, lo = split(a)
-        p = mm(jnp.concatenate([hi, lo], axis=1), xhh[s]) + mm(hi, xlo[s])
+        p = mm(jnp.concatenate([hi, lo, hi], axis=1), xs[s])
         acc[d, 0:TILE, :] += p[:, 0:TILE]
         acc[d, TILE : 2 * TILE, :] += p[:, TILE:]
         total[d] += a
@@ -138,18 +140,23 @@
 
     lax.fori_loop(0, CHUNKS, chunk, 0)
     ones = jnp.ones((8, 2 * TILE), BF16)
+    per = DESTS // 8
+
+    def write(g):
+        at = pl.ds(g * per, per)
+        return pltpu.make_async_copy(acc.at[at], out_hbm.at[at], out_sem.at[g])
 
     def degrees(g, _):
-        for u in range(4):
-            d = g * 4 + u
+        for u in range(per):
+            d = g * per + u
             hi, lo = split(total[d])
             acc[d, 2 * TILE :, :] = mm(ones, jnp.concatenate([hi, lo], axis=1), ((1,), (1,)))
+        write(g).start()
         return 0
 
-    lax.fori_loop(0, DESTS // 4, degrees, 0)
-    out = pltpu.make_async_copy(acc.at[pl.ds(0, DESTS)], out_hbm, out_sem)
-    out.start()
-    out.wait()
+    lax.fori_loop(0, 8, degrees, 0)
+    for g in range(8):
+        write(g).wait()
 
 
 def forward_tiles(dest, source, count, slab, values):
@@ -162,10 +169,9 @@
             pltpu.VMEM((SLOTS, TILE, TILE), F32),
             pltpu.VMEM((DESTS + 1, ROWS, TILE), F32),
             pltpu.VMEM((DESTS + 1, TILE, TILE), F32),
-            pltpu.VMEM((SOURCES, 2 * TILE, WIDTH), BF16),
-            pltpu.VMEM((SOURCES, TILE, WIDTH), BF16),
+            pltpu.VMEM((SOURCES, 3 * TILE, WIDTH), BF16),
             DMA((CHUNKS,)),
-            DMA,
+            DMA((8,)),
         ],
         compiler_params=pltpu.CompilerParams(vmem_limit_bytes=VMEM_LIMIT),
         cost_estimate=pl.CostEstimate(
@@ -186,7 +192,7 @@
 
 PARTS = 32
 PART_ROWS = 40
-AR_SENDS = 17
+AR_SENDS = 10
 FIRST = 64
 SUM_ROWS = (((0, 136), (136, 128)), ((FIRST, 104), (FIRST + 104, 96)))
 GATH_ROWS = (((0, 128), (128, 128)), ((FIRST, 96), (FIRST + 96, 96)))
@@ -196,7 +202,7 @@
 def exchange_kernel(
     part_hbm, x_ref, ws_ref, wn_ref, bias_ref, cot_ref,
     layer_out, direct_out, g_out, gw_out,
-    acc, relays, arrivals, zfirst, zlast, gath, own_term, gwp, gws, r1, r2, r3, r4, own_part,
+    acc, relays, arrivals, zfirst, zlast, gath, own_term, gwp, r1, r2, r3, r4, own_part,
     load_sem, rs_send, rs_recv, zs_send, zs_recv, ag_send, ag_recv, zg_send, zg_recv, ar_send, ar_recv, out_sem,
 ):
     row, col = lax.axis_index("row"), lax.axis_index("col")
@@ -330,7 +336,7 @@
         src = acc.at[(*at_place(order, 0, 0, 1, 0), rows)]
         return remote(src, zlast.at[order, rows], zs_send.at[8 + order], zs_recv.at[8 + order], z_mate)
 
-    turn = [(which, 1) for which in (2, 1, 3, 0)] + [(which, 0) for which in (2, 1, 3, 0)]
+    turn = [(2, 1), (1, 1), (3, 1), (2, 0), (0, 1), (1, 0), (3, 0), (0, 0)]
     for which, mine in turn:
         for order in range(2):
             load(order, which, mine).start()
@@ -358,29 +364,30 @@
                     acc[at] += zfirst[order, which, j]
             wide[i][order].issue()
 
-    for i in range(len(turn) + 3):
+    for i in range(len(turn) + 1):
         if i < len(turn):
             sum_issue(i)
         if i == 0:
             own_term[...] = dot3(x_ref[...], ws_ref[...])
-        if 1 <= i <= len(turn):
+        if i >= 1:
             each(wide[i - 1], "relay")
         if i == 5:
+            for n in range(3):
+                each(wide[n], "finish")
+            each(narrow[1], "issue")
+        if i == 6:
             each(narrow[1], "relay")
-        if i == 9:
-            each(narrow[0], "relay")
-        if 2 <= i <= len(turn) + 1:
-            each(wide[i - 2], "finish")
-        if i == 4:
-            each(narrow[1], "issue")
-        if i == 8:
-            each(narrow[0], "issue")
-        if i == 6:
+        if i == 7:
+            each(wide[4], "finish")
             each(narrow[1], "finish")
             for order in range(2):
                 z_last(order).start()
-        if i == 10:
-            each(narrow[0], "finish")
+    for n in (3, 5, 6):
+        each(wide[n], "finish")
+    each(narrow[0], "issue")
+    each(wide[7], "finish")
+    each(narrow[0], "relay")
+    each(narrow[0], "finish")
 
     x_own = x_ref[...]
     ws, wn = ws_ref[...], wn_ref[...]
@@ -447,19 +454,12 @@
     n_core, n_x, n_y = 16 * PART_ROWS, 4 * PART_ROWS, PART_ROWS
     rows_at = lambda c, xx, yy, n: pl.ds(pl.multiple_of((c * 16 + xx * 4 + yy) * PART_ROWS, 8), n)
     span = lambda *at: gwp.at[rows_at(*at)]
-    summed = lambda *at: gws.at[rows_at(*at)]
     hop = lambda i, src, dst, device: remote(src, dst, ar_send.at[i], ar_recv.at[i], device)
 
     c1 = [hop(0, span(1 - core, 0, 0, n_core), r1, core_mate)]
     c2 = [hop(d, span(core, ahead(x, d), 0, n_x), r2.at[d - 1], x_others[d - 1]) for d in range(1, 4)]
     c3 = [hop(3 + d, span(core, x, ahead(y, d), n_y), r3.at[d - 1], y_others[d - 1]) for d in range(1, 4)]
     c4 = [hop(7 + d, own_part, r4.at[d], z_others[d]) for d in range(3)]
-    mine = summed(core, x, y, n_y)
-    c5 = [hop(9 + d, mine, mine, y_others[d - 1]) for d in range(1, 4)]
-    mine_x = summed(core, x, 0, n_x)
-    c6 = [hop(12 + d, mine_x, mine_x, x_others[d - 1]) for d in range(1, 4)]
-    mine_c = summed(core, 0, 0, n_core)
-    c7 = [hop(16, mine_c, mine_c, core_mate)]
 
     def launch(copies):
         for c in copies:
@@ -492,25 +492,7 @@
 
     def phase4():
         land(c4)
-        gws[rows_at(core, x, y, n_y), :] = (own_part[...] + r4[0]) + (r4[1] + r4[2])
-        launch(c5)
-
-    def phase5():
-        for d in range(1, 4):
-            peer = summed(core, x, ahead(y, 4 - d), n_y)
-            hop(9 + d, peer, peer, y_others[d - 1]).wait_recv()
-        launch(c6)
-
-    def phase6():
-        for d in range(1, 4):
-            peer = summed(core, ahead(x, 4 - d), 0, n_x)
-            hop(12 + d, peer, peer, x_others[d - 1]).wait_recv()
-        launch(c7)
-
-    def phase7():
-        peer = summed(1 - core, 0, 0, n_core)
-        hop(16, peer, peer, core_mate).wait_recv()
-        gw_out[...] = gws[0 : 4 * WIDTH + 8, :]
+        gw_out[...] = (own_part[...] + r4[0]) + (r4[1] + r4[2])
 
     launch(c1)
     direct_out[...] = dot3(grad_pre, ws, ((1,), (1,)))
@@ -519,48 +501,39 @@
     each(gwide[0, 0], "relay")
     each(gnarrow[0], "near")
     each(gwide[1, 0], "issue")
-    phase1()
     for order in range(2):
         give(order, 1).wait_recv()
     each(gnarrow[1], "issue")
     each(gwide[3, 0], "issue")
     each(gwide[1, 0], "relay")
-    done(0, 0)
-    phase2()
+    phase1()
     each(gnarrow[1], "relay")
     each(gnarrow[0], "finish")
     each(gwide[2, 0], "issue")
     each(gwide[3, 0], "relay")
-    done(1, 0)
-    phase3()
+    done(0, 0)
     each(gwide[0, 1], "issue")
     each(gwide[2, 0], "relay")
-    done(3, 0)
+    done(1, 0)
     each(gnarrow[1], "near")
-    phase4()
     each(gwide[1, 1], "issue")
     each(gwide[0, 1], "relay")
-    done(2, 0)
+    done(3, 0)
+    phase2()
     each(gnarrow[1], "finish")
-    phase5()
     each(gwide[3, 1], "issue")
     each(gwide[1, 1], "relay")
-    done(0, 1)
-    phase6()
+    done(2, 0)
     each(gwide[2, 1], "issue")
     each(gwide[3, 1], "relay")
-    done(1, 1)
-    phase7()
+    phase3()
     each(gwide[2, 1], "relay")
-    done(3, 1)
-    for which in (0, 1, 3):
+    for which in (0, 1, 3, 2):
+        done(which, 1)
         for order in range(2):
             z_after(order, which, 1).wait_recv()
             write(order, which, 1).start()
-    done(2, 1)
-    for order in range(2):
-        z_after(order, 2, 1).wait_recv()
-        write(order, 2, 1).start()
+    phase4()
 
     for pair in wide + narrow + list(gwide.values()) + gnarrow:
         each(pair, "drain")
@@ -570,9 +543,6 @@
         for which in range(4):
             z_first(order, which).wait_send()
             z_after(order, which, 0).wait_send()
-    for copies in (c5, c6, c7):
-        for c in copies:
-            c.wait_send()
     for which in range(4):
         for order in range(2):
             for own_z in range(2):
@@ -588,7 +558,7 @@
             jax.ShapeDtypeStruct((n, WIDTH), F32),
             jax.ShapeDtypeStruct((n, WIDTH), F32),
             jax.ShapeDtypeStruct((*layout, 2 * TILE, TILE), F32),
-            jax.ShapeDtypeStruct((4 * WIDTH + 8, TILE), F32),
+            jax.ShapeDtypeStruct((PART_ROWS, TILE), F32),
         ),
         in_specs=[ANY, VM, VM, VM, VM, VM],
         out_specs=(VM, VM, ANY, VM),
@@ -600,7 +570,6 @@
             pltpu.VMEM((2, ROWS, TILE), F32),
             pltpu.VMEM((*layout, 2 * TILE, TILE), F32),
             pltpu.VMEM((n, WIDTH), F32),
-            pltpu.VMEM((PARTS * PART_ROWS, TILE), F32),
             pltpu.VMEM((PARTS * PART_ROWS, TILE), F32),
             pltpu.VMEM((16 * PART_ROWS, TILE), F32),
             pltpu.VMEM((3, 4 * PART_ROWS, TILE), F32),
@@ -629,11 +598,15 @@
     return layer_out, direct, g.reshape(DESTS, 2 * TILE, TILE), gw
 
 
-def backward_kernel(dest, source, count, g_hbm, tiles_hbm, out_ref, tiles, g, ghh, glo, acc, sems, g_sem):
+def backward_kernel(
+    dest, source, count, g_hbm, tiles_hbm, kept_hbm, out_ref, kept_out, tiles, g, acc, sems, g_sem, kept_sem
+):
     g_copy = pltpu.make_async_copy(g_hbm, g, g_sem)
     g_copy.start()
     for c in range(CHUNKS):
         tile_copy(tiles_hbm, tiles, sems, c).start()
+    kept = pltpu.make_async_copy(kept_hbm, kept_out, kept_sem)
+    kept.start()
     live = count[0]
 
     def clear(s, _):
@@ -642,24 +615,14 @@
 
     lax.fori_loop(0, SOURCES + 1, clear, 0)
     g_copy.wait()
-
-    def cut(d, _):
-        for half in range(2):
-            hi, lo = split(g[d, half * TILE : (half + 1) * TILE, :])
-            lanes = slice(half * TILE, (half + 1) * TILE)
-            ghh[d, 0:TILE, lanes] = hi
-            ghh[d, TILE:, lanes] = hi
-            glo[d, :, lanes] = lo
-        return 0
-
-    lax.fori_loop(0, DESTS, cut, 0)
 
     def one(t):
         d = dest[t]
         s = jnp.where(t < live, source[t], SOURCES)
         hi, lo = split(tiles[t])
-        p = mm(jnp.concatenate([hi, lo], axis=0), ghh[d], ((0,), (0,))) + mm(hi, glo[d], ((0,), (0,)))
-        acc[s] += p
+        ghi, glo = split(jnp.concatenate([g[d, 0:TILE, :], g[d, TILE:, :]], axis=1))
+        a = jnp.concatenate([hi, lo, hi], axis=0)
+        acc[s] += mm(a, jnp.concatenate([ghi, ghi, glo], axis=0), ((0,), (0,)))
 
     def group(g_, _):
         for u in range(UNROLL):
@@ -674,21 +637,21 @@
     lax.fori_loop(0, CHUNKS, chunk, 0)
     for s in range(SOURCES):
         out_ref[s * TILE : (s + 1) * TILE, :] = acc[s]
-
-
-def backward_tiles(dest, source, count, g, values):
+    kept.wait()
+
+
+def backward_tiles(dest, source, count, g, values, kept):
     return pl.pallas_call(
         backward_kernel,
-        out_shape=jax.ShapeDtypeStruct((SOURCES * TILE, WIDTH), F32),
-        in_specs=[SM, SM, SM, ANY, ANY],
-        out_specs=VM,
+        out_shape=(jax.ShapeDtypeStruct((SOURCES * TILE, WIDTH), F32), jax.ShapeDtypeStruct(kept.shape, F32)),
+        in_specs=[SM, SM, SM, ANY, ANY, ANY],
+        out_specs=(VM, ANY),
         scratch_shapes=[
             pltpu.VMEM((SLOTS, TILE, TILE), F32),
             pltpu.VMEM((DESTS, 2 * TILE, TILE), F32),
-            pltpu.VMEM((DESTS, 2 * TILE, WIDTH), BF16),
-            pltpu.VMEM((DESTS, TILE, WIDTH), BF16),
             pltpu.VMEM((SOURCES + 1, TILE, WIDTH), F32),
             DMA((CHUNKS,)),
+            DMA,
             DMA,
         ],
         compiler_params=pltpu.CompilerParams(vmem_limit_bytes=VMEM_LIMIT),
@@ -696,52 +659,86 @@
             flops=SLOTS * 6 * TILE * TILE * WIDTH, bytes_accessed=22_000_000, transcendentals=0
         ),
         name="backward_tiles",
-    )(dest, source, count, g, values)
-
-
-def scatter_kernel(back_ref, direct_ref, out_ref, near, cross, send_buf, send, recv):
+    )(dest, source, count, g, values, kept)
+
+
+def scatter_kernel(back_ref, part_ref, out_ref, gw_out, near, cross, send_buf, gws, send, recv, ar_send, ar_recv):
     row, col = lax.axis_index("row"), lax.axis_index("col")
     hi, core = lax.div(row, 2), lax.rem(row, 2)
-    mate = hi * 2 + (1 - core)
-    far = (1 - hi) * 2 + core
-    far_mate = (1 - hi) * 2 + (1 - core)
-    enter([(mate, col), (far, col)])
-    n = direct_ref.shape[0]
-    at = lambda r: pl.ds(pl.multiple_of(r * n, n), n)
-    first = remote(back_ref.at[at(far_mate)], near.at[0], send.at[0], recv.at[0], (mate, col))
-    first.start()
-    second = remote(back_ref.at[at(mate)], near.at[1], send.at[1], recv.at[1], (mate, col))
-    second.start()
-    first.wait_recv()
-    send_buf[...] = back_ref[at(far), :] + near[0]
-    third = remote(send_buf, cross, send.at[2], recv.at[2], (far, col))
-    third.start()
-    second.wait_recv()
-    total = direct_ref[...] + back_ref[at(row), :] + near[1]
-    third.wait_recv()
-    out_ref[...] = total + cross[...]
-    first.wait_send()
-    second.wait_send()
-    third.wait_send()
-
-
-def scatter_rows(back, direct):
-    n = direct.shape[0]
+    x, y, z = lax.div(col, 8), lax.rem(lax.div(col, 2), 4), lax.rem(col, 2)
+    column = lambda xx, yy, zz: xx * 8 + yy * 2 + zz
+    ahead = lambda p, d: lax.rem(p + d, 4)
+    x_others = [(row, column(ahead(x, d), y, z)) for d in range(1, 4)]
+    y_others = [(row, column(x, ahead(y, d), z)) for d in range(1, 4)]
+    mate = (hi * 2 + (1 - core), col)
+    far = ((1 - hi) * 2 + core, col)
+    enter([mate, far] + x_others + y_others)
+    n = out_ref.shape[0]
+    m = n // PIECES
+    at = lambda r, c: pl.ds(pl.multiple_of(r * n + c * m, m), m)
+    piece = lambda c: pl.ds(c * m, m)
+    far_row, far_mate = (1 - hi) * 2 + core, (1 - hi) * 2 + (1 - core)
+    first, second, third = [], [], []
+    for c in range(PIECES):
+        src = back_ref.at[at(far_mate, c)]
+        first.append(remote(src, near.at[0, piece(c)], send.at[0, c], recv.at[0, c], mate))
+        src = back_ref.at[at(hi * 2 + (1 - core), c)]
+        second.append(remote(src, near.at[1, piece(c)], send.at[1, c], recv.at[1, c], mate))
+        third.append(remote(send_buf.at[piece(c)], cross.at[piece(c)], send.at[2, c], recv.at[2, c], far))
+    for c in first + second:
+        c.start()
+
+    rows_at = lambda c, xx, yy, k: pl.ds(pl.multiple_of((c * 16 + xx * 4 + yy) * PART_ROWS, 8), k)
+    summed = lambda *w: gws.at[rows_at(*w)]
+    hop = lambda i, ref, device: remote(ref, ref, ar_send.at[i], ar_recv.at[i], device)
+    gws[rows_at(core, x, y, PART_ROWS), :] = part_ref[...]
+    c5 = [hop(d, summed(core, x, y, PART_ROWS), y_others[d]) for d in range(3)]
+    c6 = [hop(3 + d, summed(core, x, 0, 4 * PART_ROWS), x_others[d]) for d in range(3)]
+    c7 = [hop(6, summed(core, 0, 0, 16 * PART_ROWS), mate)]
+    for c in c5:
+        c.start()
+    for c in range(PIECES):
+        first[c].wait_recv()
+        send_buf[piece(c), :] = back_ref[at(far_row, c), :] + near[0, piece(c), :]
+        third[c].start()
+    for d in range(3):
+        hop(d, summed(core, x, ahead(y, 3 - d), PART_ROWS), y_others[d]).wait_recv()
+    for c in c6:
+        c.start()
+    for d in range(3):
+        hop(3 + d, summed(core, ahead(x, 3 - d), 0, 4 * PART_ROWS), x_others[d]).wait_recv()
+    for c in c7:
+        c.start()
+    for c in range(PIECES):
+        second[c].wait_recv()
+        third[c].wait_recv()
+        out_ref[piece(c), :] = back_ref[at(row, c), :] + near[1, piece(c), :] + cross[piece(c), :]
+    hop(6, summed(1 - core, 0, 0, 16 * PART_ROWS), mate).wait_recv()
+    gw_out[...] = gws[0 : 4 * WIDTH + 8, :]
+    for c in first + second + third + c5 + c6 + c7:
+        c.wait_send()
+
+
+def scatter_rows(back, part):
+    n = back.shape[0] // 4
     return pl.pallas_call(
         scatter_kernel,
-        out_shape=jax.ShapeDtypeStruct((n, WIDTH), F32),
+        out_shape=(jax.ShapeDtypeStruct((n, WIDTH), F32), jax.ShapeDtypeStruct((4 * WIDTH + 8, TILE), F32)),
         in_specs=[VM, VM],
-        out_specs=VM,
+        out_specs=(VM, VM),
         scratch_shapes=[
             pltpu.VMEM((2, n, WIDTH), F32),
             pltpu.VMEM((n, WIDTH), F32),
             pltpu.VMEM((n, WIDTH), F32),
-            DMA((3,)),
-            DMA((3,)),
+            pltpu.VMEM((PARTS * PART_ROWS, TILE), F32),
+            DMA((3, PIECES)),
+            DMA((3, PIECES)),
+            DMA((7,)),
+            DMA((7,)),
         ],
         compiler_params=pltpu.CompilerParams(collective_id=2, has_side_effects=True),
         name="scatter_rows",
-    )(back, direct)
+    )(back, part)
 
 
 def body(x, ws, wn, bias, tile_values, tile_dest, tile_source, tile_count, cot):
@@ -749,9 +746,10 @@
     dest, source, count = tile_dest.reshape(SLOTS), tile_source.reshape(SLOTS), tile_count.reshape(1)
     slab = gather_rows(x)
     part = forward_tiles(dest, source, count, slab, values)
-    layer_out, direct, g, gw = exchange(part, x, ws, wn, bias, cot)
-    back = backward_tiles(dest, source, count, g, values)
-    grad_x = scatter_rows(back, direct)
+    layer_out, direct, g, gw_part = exchange(part, x, ws, wn, bias, cot)
+    back, layer_out = backward_tiles(dest, source, count, g, values, layer_out)
+    back, gw = scatter_rows(back, gw_part)
+    grad_x = direct + back
     w = lambda i: jnp.concatenate([gw[i * WIDTH : (i + 1) * WIDTH], gw[(i + 1) * WIDTH : (i + 2) * WIDTH]], axis=1)
     grad_bias = gw[4 * WIDTH : 4 * WIDTH + 2].reshape(WIDTH)
     return layer_out, grad_x, w(0), w(2), grad_bias

time: 180 us -> 172 us (0.956)
  Pallas kernels: 175 us -> 165 us
    pallas_call x1, Pallas kernels: 106 us -> 96.3 us  [exchange(): pl.pallas_call(exchange_kernel, out_shape=(jax.ShapeDtypeStruct((n, WIDTH...]
    pallas_call x2, Pallas kernels: 34.1 us -> 37.3 us  [the longest x1 19.3 us: scatter_rows(): pl.pallas_call(scatter_kernel, out_shape=(jax.ShapeDtypeStruct((n, WIDTH)...]
    pallas_call x1, Pallas kernels: 19 us -> 16 us  [forward_tiles(): pl.pallas_call(forward_kernel, out_shape=jax.ShapeDtypeStruct((DESTS, ROW...]
    unnamed x6 -> x2, local copies, waits for them, and re-layouts: 2.38 us -> 0.01 us
where the time goes in v3:
time: 172 us; the launch traced here: 171 us
  Pallas kernels  165 us (96%)
  other arithmetic  2.51 us (1%)
  local copies, waits for them, and re-layouts  2.38 us (1%)
    pallas_call x1, Pallas kernels, exchange(): pl.pallas_call(exchange_kernel, out_shape=(jax.ShapeDtypeStruct((n, WIDTH...  96.3 us
    pallas_call x1, Pallas kernels, scatter_rows(): pl.pallas_call(scatter_kernel, out_shape=(jax.ShapeDtypeStruct((n, WIDTH)...  19.3 us
    pallas_call x1, Pallas kernels, backward_tiles(): pl.pallas_call(backward_kernel, out_shape=(jax.ShapeDtypeStruct((SOURCES...  18 us
    pallas_call x1, Pallas kernels, forward_tiles(): pl.pallas_call(forward_kernel, out_shape=jax.ShapeDtypeStruct((DESTS, ROW...  16 us
    pallas_call x1, Pallas kernels, gather_rows(): pl.pallas_call(gather_kernel, out_shape=jax.ShapeDtypeStruct((4 * x.shape...  15.4 us

profile of v3, /device:TPU:1, one launch (start us, length us, event | category | flops | bytes accessed | tf_op | source)
XLA Modules:
  0.0 171.3 jit_solution(6313068775744341068)
XLA Ops:
  1.3 15.4 %gather_rows.1.x_ref = f32[1024,256]{1,0:T(8,128)} custom-call(f32[256,256]{1,0:T(8,128)} %x_ref.3), custom_call_target="tpu_custom_call" | custom-call | tf_op jit(solution)/shard_map/gather_rows/pallas_call | solution.py:88
  16.7 16.0 %forward_tiles.1 = f32[64,264,128]{2,1,0:T(8,128)} custom-call(s32[192]{0:T(256)} %bitcast.15, s32[192]{0:T(256)} %bitcast.17, s32[1]{0:T(128)} %bitcast.9.count, f32[1024,256]{1,0:T(8,128)} %gather_rows.1.x_ref, f32[192,128,128]{2,1,0:T(8,128)} %bitcast.11), custom_call_target="tpu_custom_call" | custom-call | flops 4831838208 | bytes 22000000 | tf_op jit(solution)/shard_map/forward_tiles/pallas_call | solution.py:163
  32.7 96.3 %exchange.1 = (f32[256,256]{1,0:T(8,128)}, f32[256,256]{1,0:T(8,128)}, f32[4,4,2,2,256,128]{5,4,3,2,1,0:T(8,128)}, f32[40,128]{1,0:T(8,128)}) custom-call(f32[4,4,2,2,264,128]{5,4,3,2,1,0:T(8,128)} %bitcast.13, f32[256,256]{1,0:T(8,128)} %x_ref.3, f32[256,256]{1,0:T(8,128)} %ws_ref.1, f32[256,256]{1,0:T(8,128)} %wn_ref.1, f32[1,256]{1,0:T(1,128)} %bitcast.19, ...), custom_call_target="tpu_custom_call" | custom-call | tf_op jit(solution)/shard_map/exchange/pallas_call | solution.py:555
  129.1 0.0 copy-start
  129.1 18.0 %backward_tiles.1 = (f32[1024,256]{1,0:T(8,128)}, f32[256,256]{1,0:T(8,128)}) custom-call(s32[192]{0:T(256)} %bitcast.16, s32[192]{0:T(256)} %bitcast.18, s32[1]{0:T(128)} %bitcast.10.count, f32[64,256,128]{2,1,0:T(8,128)} %bitcast.14, f32[192,128,128]{2,1,0:T(8,128)} %bitcast.12, f32[256,256]{1,0:T(8,128)} %get-tuple-element.14.kept_hbm), custom_call_target="tpu_custom_call" | custom-call | flops 4831838208 | bytes 22000000 | tf_op jit(solution)/shard_map/backward_tiles/pallas_call | solution.py:644
  147.1 19.3 %scatter_rows.1 = (f32[256,256]{1,0:T(8,128)}, f32[1032,128]{1,0:T(8,128)}) custom-call(f32[1024,256]{1,0:T(8,128)} %get-tuple-element.17.back_ref, f32[40,128]{1,0:T(8,128)} %get-tuple-element.18.part_ref), custom_call_target="tpu_custom_call" | custom-call | tf_op jit(solution)/shard_map/scatter_rows/pallas_call | solution.py:724
  166.4 0.0 copy-done
  166.4 1.7 add.3
  168.1 1.2 slice_bitcast_fusion
  169.3 1.1 fusion
  170.5 0.8 pad_maximum_fusion
Async XLA Ops:
  129.1 37.3 %copy-start = (f32[256,256]{1,0:T(8,128)S(1)}, f32[256,256]{1,0:T(8,128)}, u32[]{:S(2)}) copy-start(f32[256,256]{1,0:T(8,128)} %get-tuple-element.16) | copy-start | bytes 786436

commit v4 on v3

--- a/solution.py
+++ b/solution.py
@@ -21,6 +21,13 @@
 CHUNKS = SLOTS // CHUNK
 UNROLL = 16
 PIECES = 4
+FIT = 8
+KEYS = 4 * SOURCES
+PLAN_TILE, PLAN_BLOCK, PLAN_COUNT = 0, KEYS * FIT, 2 * KEYS * FIT
+PLAN_REST, PLAN_LIST = PLAN_COUNT + KEYS, PLAN_COUNT + 2 * KEYS
+PLAN_SIZE = 1024
+PLAN_VOID = PLAN_SIZE - 1
+REST_SLOTS = 16
 VMEM_LIMIT = 60 * 1024 * 1024
 
 VM = pl.BlockSpec(memory_space=pltpu.VMEM)
@@ -57,7 +64,18 @@
     )
 
 
-def gather_kernel(x_ref, out_ref, local_sem, send, recv):
+def arrival(q, col):
+    x, y, z = lax.div(col, 8), lax.rem(lax.div(col, 2), 4), lax.rem(col, 2)
+    bx, by, order = lax.shift_right_logical(q, 4), lax.shift_right_logical(q, 2) & 3, q & 1
+    other = (lax.shift_right_logical(q, 1) & 1) ^ z
+    which = jnp.where(order == 0, by - y, bx - x) & 3
+    wide = jnp.where(order == 0, bx, by)
+    half = lax.shift_right_logical(which, 1)
+    local = (which & 1) ^ half
+    return other * 2 + half, (local * 4 + wide) * 2 + order
+
+
+def gather_kernel(count, dest_ref, source_ref, x_ref, out_ref, keys_out, local_sem, send, recv):
     row, col = lax.axis_index("row"), lax.axis_index("col")
     hi, core = lax.div(row, 2), lax.rem(row, 2)
     mate = hi * 2 + (1 - core)
@@ -74,6 +92,11 @@
     for c in across + beside:
         c.start()
     own.start()
+    dest = dest_ref[...]
+    quarter, block = arrival(dest, col)
+    listed = lax.broadcasted_iota(jnp.int32, dest.shape, 1) < count[0]
+    keys_out[0:1, :] = jnp.where(listed, quarter * SOURCES + source_ref[...], KEYS)
+    keys_out[1:2, :] = quarter * 16 + block
     for c in range(PIECES):
         across[c].wait_recv()
         onward[c].start()
@@ -84,16 +107,16 @@
         c.wait_send()
 
 
-def gather_rows(x):
+def gather_rows(count, dest, source, x):
     return pl.pallas_call(
         gather_kernel,
-        out_shape=jax.ShapeDtypeStruct((4 * x.shape[0], x.shape[1]), F32),
-        in_specs=[VM],
-        out_specs=VM,
+        out_shape=(jax.ShapeDtypeStruct((4 * x.shape[0], x.shape[1]), F32), jax.ShapeDtypeStruct((2, SLOTS), jnp.int32)),
+        in_specs=[SM, VM, VM, VM],
+        out_specs=(VM, VM),
         scratch_shapes=[DMA, DMA((3, PIECES)), DMA((3, PIECES))],
         compiler_params=pltpu.CompilerParams(collective_id=0, has_side_effects=True),
         name="gather_rows",
-    )(x)
+    )(count, dest, source, x)
 
 
 def tile_copy(tiles_hbm, tiles, sems, c):
@@ -101,7 +124,9 @@
     return pltpu.make_async_copy(tiles_hbm.at[at], tiles.at[at], sems.at[c])
 
 
-def forward_kernel(dest, source, count, x_ref, tiles_hbm, out_hbm, tiles, acc, total, xs, sems, out_sem):
+def forward_kernel(
+    dest, source, keys, count, x_ref, tiles_hbm, out_hbm, plan, tiles, acc, total, xs, held, sems, out_sem
+):
     for c in range(CHUNKS):
         tile_copy(tiles_hbm, tiles, sems, c).start()
     live = count[0]
@@ -114,13 +139,28 @@
     def clear(d, _):
         acc[d] = jnp.zeros((ROWS, TILE), F32)
         total[d] = jnp.zeros((TILE, TILE), F32)
+        for u in range(2 * KEYS * FIT // DESTS):
+            plan[jnp.minimum(d, DESTS - 1) * (2 * KEYS * FIT // DESTS) + u] = 0
+        held[jnp.minimum(d, KEYS + 1)] = 0
         return 0
 
     lax.fori_loop(0, DESTS + 1, clear, 0)
 
+    def enlist(t):
+        key = keys[0, t]
+        n, rest = held[key], held[KEYS + 1]
+        late = jnp.logical_and(key < KEYS, n >= FIT)
+        fits = jnp.logical_and(key < KEYS, n < FIT)
+        slot = jnp.where(fits, key * FIT + n, PLAN_VOID - PLAN_BLOCK)
+        plan[jnp.where(late, PLAN_LIST + rest, PLAN_TILE + slot)] = t
+        plan[PLAN_BLOCK + slot] = keys[1, t]
+        held[key] = n + 1
+        held[KEYS + 1] = rest + jnp.where(late, 1, 0)
+
     def one(t):
-        s = source[t]
-        d = jnp.where(t < live, dest[t], DESTS)
+        enlist(t)
+        s = source[0, t]
+        d = jnp.where(t < live, dest[0, t], DESTS)
         a = tiles[t]
         hi, lo = split(a)
         p = mm(jnp.concatenate([hi, lo, hi], axis=1), xs[s])
@@ -155,21 +195,29 @@
         return 0
 
     lax.fori_loop(0, 8, degrees, 0)
+
+    def counts(k, _):
+        plan[PLAN_COUNT + k] = jnp.minimum(held[k], FIT)
+        return 0
+
+    lax.fori_loop(0, KEYS, counts, 0)
+    plan[PLAN_REST] = held[KEYS + 1]
     for g in range(8):
         write(g).wait()
 
 
-def forward_tiles(dest, source, count, slab, values):
+def forward_tiles(dest, source, keys, count, slab, values):
     return pl.pallas_call(
         forward_kernel,
-        out_shape=jax.ShapeDtypeStruct((DESTS, ROWS, TILE), F32),
-        in_specs=[SM, SM, SM, VM, ANY],
-        out_specs=ANY,
+        out_shape=(jax.ShapeDtypeStruct((DESTS, ROWS, TILE), F32), jax.ShapeDtypeStruct((PLAN_SIZE,), jnp.int32)),
+        in_specs=[SM, SM, SM, SM, VM, ANY],
+        out_specs=(ANY, SM),
         scratch_shapes=[
             pltpu.VMEM((SLOTS, TILE, TILE), F32),
             pltpu.VMEM((DESTS + 1, ROWS, TILE), F32),
             pltpu.VMEM((DESTS + 1, TILE, TILE), F32),
             pltpu.VMEM((SOURCES, 3 * TILE, WIDTH), BF16),
+            pltpu.SMEM((KEYS + 2,), jnp.int32),
             DMA((CHUNKS,)),
             DMA((8,)),
         ],
@@ -178,7 +226,7 @@
             flops=SLOTS * 6 * TILE * TILE * WIDTH, bytes_accessed=22_000_000, transcendentals=0
         ),
         name="forward_tiles",
-    )(dest, source, count, slab, values)
+    )(dest, source, keys, count, slab, values)
 
 
 def rms_silu(pre, cot):
@@ -200,11 +248,12 @@
 
 
 def exchange_kernel(
-    part_hbm, x_ref, ws_ref, wn_ref, bias_ref, cot_ref,
-    layer_out, direct_out, g_out, gw_out,
-    acc, relays, arrivals, zfirst, zlast, gath, own_term, gwp, r1, r2, r3, r4, own_part,
-    load_sem, rs_send, rs_recv, zs_send, zs_recv, ag_send, ag_recv, zg_send, zg_recv, ar_send, ar_recv, out_sem,
+    plan, part_hbm, x_ref, ws_ref, wn_ref, bias_ref, cot_ref, tiles_hbm,
+    layer_out, direct_out, g_out, gw_out, back_out,
+    acc, relays, arrivals, zfirst, zlast, g0, g1, g2, g3, tiles, own_term, gwp, r1, r2, r3, r4, own_part,
+    load_sem, rs_send, rs_recv, zs_send, zs_recv, ag_send, ag_recv, zg_send, zg_recv, ar_send, ar_recv, out_sem, tile_sem,
 ):
+    quarters = (g0, g1, g2, g3)
     row, col = lax.axis_index("row"), lax.axis_index("col")
     zh, core = lax.div(row, 2), lax.rem(row, 2)
     x, y, z = lax.div(col, 8), lax.rem(lax.div(col, 2), 4), lax.rem(col, 2)
@@ -275,10 +324,21 @@
             for c in self.copies:
                 c.wait_send()
 
+    def quarter_of(which, mine):
+        return mine * 2 + which // 2, (which & 1) ^ (which // 2)
+
+    def held(order, wide, which, mine):
+        quarter, local = quarter_of(which, mine)
+        return quarters[quarter].at[local, wide, order]
+
     class Gather:
         def __init__(self, order, w, which, mine):
             n = number(order, w, which, mine)
-            blk = lambda j: at_place(order, w, which, mine, j % 4)
+            p = x if order == 0 else y
+
+            def blk(j):
+                return held(order, ahead(p, j), which, mine) if w == 0 else held(order, p, j, mine)
+
             top, low = GATH_ROWS[mine]
             up, down = ring(order, w)
             self.out, self.come = [], []
@@ -292,9 +352,10 @@
                     (1, 2, low, down),
                 )
             ):
-                for j, kept in ((leaves, self.out), (comes, self.come)):
-                    ref = gath.at[(*blk(j), pl.ds(*rows))]
-                    kept.append(remote(ref, ref, ag_send.at[n, i], ag_recv.at[n, i], device))
+                src, come = blk(leaves).at[pl.ds(*rows)], blk(comes).at[pl.ds(*rows)]
+                dst = src if w == 0 else come
+                self.out.append(remote(src, dst, ag_send.at[n, i], ag_recv.at[n, i], device))
+                self.come.append(remote(come, come, ag_send.at[n, i], ag_recv.at[n, i], device))
 
         def issue(self):
             for c in self.out[:4]:
@@ -340,6 +401,8 @@
     for which, mine in turn:
         for order in range(2):
             load(order, which, mine).start()
+    tile_load = pltpu.make_async_copy(tiles_hbm, tiles, tile_sem)
+    tile_load.start()
     enter([core_mate] + x_others + y_others + z_others)
     for which in (2, 1, 3, 0):
         for order in range(2):
@@ -408,22 +471,43 @@
     spread = dot3(grad_pre, wn, ((1,), (1,))) * inv
     for order in range(2):
         for half in range(2):
-            gath[(*at_place(order, 0, 0, 0, 0), pl.ds(half * TILE, TILE), slice(None))] = spread[
+            held(order, x if order == 0 else y, 0, 0)[half * TILE : (half + 1) * TILE, :] = spread[
                 order * TILE : (order + 1) * TILE, half * TILE : (half + 1) * TILE
             ]
 
-    def give(order, mine):
-        ref = gath.at[(*at_place(order, 0, 0, mine, 0), pl.ds(FIRST, 2 * TILE - FIRST))]
-        return remote(ref, ref, zg_send.at[8 + order], zg_recv.at[8 + order], z_mate)
-
-    def z_after(order, which, mine):
-        ref = strip(gath, order, which, mine, (0, FIRST))
+    def give(order):
+        src, dst = [held(order, x if order == 0 else y, 0, mine).at[pl.ds(FIRST, 2 * TILE - FIRST)] for mine in range(2)]
+        return remote(src, dst, zg_send.at[8 + order], zg_recv.at[8 + order], z_mate)
+
+    def strip_held(order, which, mine):
+        quarter, local = quarter_of(which, mine)
+        return quarters[quarter].at[local, :, order]
+
+    def z_after(order, which):
         i = order * 4 + which
-        return remote(ref, ref, zg_send.at[i], zg_recv.at[i], z_mate)
+        src, dst = [strip_held(order, which, mine).at[:, pl.ds(0, FIRST)] for mine in range(2)]
+        return remote(src, dst, zg_send.at[i], zg_recv.at[i], z_mate)
 
     def write(order, which, mine):
         n = order * 8 + mine * 4 + which
-        return pltpu.make_async_copy(strip(gath, order, which, mine), strip(g_out, order, which, mine), out_sem.at[n])
+        quarter, local = quarter_of(which, mine)
+        return pltpu.make_async_copy(strip_held(order, which, mine), g_out.at[quarter, local, :, order], out_sem.at[n])
+
+    def products(quarter, sources):
+        for s in sources:
+            key = quarter * SOURCES + s
+            n = plan[PLAN_COUNT + key]
+            total = None
+            for i in range(FIT):
+                t, b = plan[PLAN_TILE + key * FIT + i], plan[PLAN_BLOCK + key * FIT + i]
+                a = tiles[t] * jnp.where(i < n, 1.0, 0.0)
+                hi, lo = split(a)
+                g = quarters[quarter][lax.shift_right_logical(b, 3) & 1, lax.shift_right_logical(b, 1) & 3, b & 1]
+                ghi, glo = split(jnp.concatenate([g[0:TILE], g[TILE:]], axis=1))
+                p = mm(jnp.concatenate([hi, lo, hi], axis=0), jnp.concatenate([ghi, ghi, glo], axis=0), ((0,), (0,)))
+                total = p if total is None else total + p
+            at = slice(s * TILE, (s + 1) * TILE)
+            back_out[at, :] = total if quarter == 0 else back_out[at, :] + total
 
     gwide = {(which, mine): [Gather(order, 0, which, mine) for order in range(2)] for which in range(4) for mine in range(2)}
     gnarrow = [[Gather(order, 1, 0, mine) for order in range(2)] for mine in range(2)]
@@ -433,11 +517,11 @@
         each(gwide[which, mine], "finish")
         for order in range(2):
             if mine == 0:
-                z_after(order, which, 0).start()
+                z_after(order, which).start()
                 write(order, which, 0).start()
 
     for order in range(2):
-        give(order, 0).start()
+        give(order).start()
     each(gnarrow[0], "issue")
     each(gwide[0, 0], "issue")
 
@@ -502,7 +586,7 @@
     each(gnarrow[0], "near")
     each(gwide[1, 0], "issue")
     for order in range(2):
-        give(order, 1).wait_recv()
+        give(order).wait_recv()
     each(gnarrow[1], "issue")
     each(gwide[3, 0], "issue")
     each(gwide[1, 0], "relay")
@@ -518,38 +602,47 @@
     each(gnarrow[1], "near")
     each(gwide[1, 1], "issue")
     each(gwide[0, 1], "relay")
+    tile_load.wait()
+    products(0, (0, 1, 2))
     done(3, 0)
     phase2()
     each(gnarrow[1], "finish")
     each(gwide[3, 1], "issue")
     each(gwide[1, 1], "relay")
+    products(0, (3, 4, 5))
     done(2, 0)
     each(gwide[2, 1], "issue")
     each(gwide[3, 1], "relay")
+    products(0, (6, 7))
     phase3()
     each(gwide[2, 1], "relay")
-    for which in (0, 1, 3, 2):
+    products(1, (0, 1, 2, 3))
+    for which in range(4):
+        if which == 2:
+            products(1, (4, 5, 6, 7))
+            products(2, range(SOURCES))
         done(which, 1)
         for order in range(2):
-            z_after(order, which, 1).wait_recv()
+            z_after(order, which).wait_recv()
             write(order, which, 1).start()
+    products(3, range(SOURCES))
     phase4()
 
     for pair in wide + narrow + list(gwide.values()) + gnarrow:
         each(pair, "drain")
     for order in range(2):
         z_last(order).wait_send()
-        give(order, 0).wait_send()
+        give(order).wait_send()
         for which in range(4):
             z_first(order, which).wait_send()
-            z_after(order, which, 0).wait_send()
+            z_after(order, which).wait_send()
     for which in range(4):
         for order in range(2):
             for own_z in range(2):
                 write(order, which, own_z).wait()
 
 
-def exchange(part, x, ws, wn, bias, cot):
+def exchange(plan, part, x, ws, wn, bias, cot, values):
     n = x.shape[0]
     layout = (4, 4, 2, 2)
     out = pl.pallas_call(
@@ -557,18 +650,20 @@
         out_shape=(
             jax.ShapeDtypeStruct((n, WIDTH), F32),
             jax.ShapeDtypeStruct((n, WIDTH), F32),
-            jax.ShapeDtypeStruct((*layout, 2 * TILE, TILE), F32),
+            jax.ShapeDtypeStruct((4, 2, 4, 2, 2 * TILE, TILE), F32),
             jax.ShapeDtypeStruct((PART_ROWS, TILE), F32),
+            jax.ShapeDtypeStruct((SOURCES * TILE, WIDTH), F32),
         ),
-        in_specs=[ANY, VM, VM, VM, VM, VM],
-        out_specs=(VM, VM, ANY, VM),
+        in_specs=[SM, ANY, VM, VM, VM, VM, VM, ANY],
+        out_specs=(VM, VM, ANY, VM, VM),
         scratch_shapes=[
             pltpu.VMEM((*layout, ROWS, TILE), F32),
             pltpu.VMEM((SLICES, 2, 136, TILE), F32),
             pltpu.VMEM((SLICES, 2, ROWS, TILE), F32),
             pltpu.VMEM((2, 4, 4, FIRST, TILE), F32),
             pltpu.VMEM((2, ROWS, TILE), F32),
-            pltpu.VMEM((*layout, 2 * TILE, TILE), F32),
+            *[pltpu.VMEM((2, 4, 2, 2 * TILE, TILE), F32) for _ in range(4)],
+            pltpu.VMEM((SLOTS, TILE, TILE), F32),
             pltpu.VMEM((n, WIDTH), F32),
             pltpu.VMEM((PARTS * PART_ROWS, TILE), F32),
             pltpu.VMEM((16 * PART_ROWS, TILE), F32),
@@ -588,78 +683,72 @@
             DMA((AR_SENDS,)),
             DMA((AR_SENDS,)),
             DMA((16,)),
+            DMA,
         ],
         compiler_params=pltpu.CompilerParams(
             collective_id=1, has_side_effects=True, vmem_limit_bytes=VMEM_LIMIT
         ),
         name="exchange",
-    )(part.reshape(*layout, ROWS, TILE), x, ws, wn, bias.reshape(1, WIDTH), cot)
-    layer_out, direct, g, gw = out
-    return layer_out, direct, g.reshape(DESTS, 2 * TILE, TILE), gw
-
-
-def backward_kernel(
-    dest, source, count, g_hbm, tiles_hbm, kept_hbm, out_ref, kept_out, tiles, g, acc, sems, g_sem, kept_sem
+    )(plan, part.reshape(*layout, ROWS, TILE), x, ws, wn, bias.reshape(1, WIDTH), cot, values)
+    layer_out, direct, g, gw, back = out
+    return layer_out, direct, g.reshape(DESTS, 2 * TILE, TILE), gw, back
+
+
+def rest_kernel(
+    plan, source, keys, g_hbm, tiles_hbm, back_ref, out_ref, tiles, g, tile_sem, g_sem
 ):
-    g_copy = pltpu.make_async_copy(g_hbm, g, g_sem)
-    g_copy.start()
-    for c in range(CHUNKS):
-        tile_copy(tiles_hbm, tiles, sems, c).start()
-    kept = pltpu.make_async_copy(kept_hbm, kept_out, kept_sem)
-    kept.start()
-    live = count[0]
-
-    def clear(s, _):
-        acc[s] = jnp.zeros((TILE, WIDTH), F32)
+    n = plan[PLAN_REST]
+
+    def copies(i):
+        slot = lax.rem(i, REST_SLOTS)
+        t = plan[PLAN_LIST + i]
+        return (
+            pltpu.make_async_copy(tiles_hbm.at[t], tiles.at[slot], tile_sem.at[slot]),
+            pltpu.make_async_copy(g_hbm.at[keys[1, t]], g.at[slot], g_sem.at[slot]),
+        )
+
+    def begin(i, _):
+        for c in copies(i):
+            c.start()
         return 0
 
-    lax.fori_loop(0, SOURCES + 1, clear, 0)
-    g_copy.wait()
-
-    def one(t):
-        d = dest[t]
-        s = jnp.where(t < live, source[t], SOURCES)
-        hi, lo = split(tiles[t])
-        ghi, glo = split(jnp.concatenate([g[d, 0:TILE, :], g[d, TILE:, :]], axis=1))
+    lax.fori_loop(0, jnp.minimum(n, REST_SLOTS), begin, 0)
+    out_ref[...] = back_ref[...]
+
+    def one(i, _):
+        for c in copies(i):
+            c.wait()
+        slot = lax.rem(i, REST_SLOTS)
+        rows = pl.ds(pl.multiple_of(source[0, plan[PLAN_LIST + i]] * TILE, TILE), TILE)
+        hi, lo = split(tiles[slot])
+        ghi, glo = split(jnp.concatenate([g[slot, 0:TILE, :], g[slot, TILE:, :]], axis=1))
         a = jnp.concatenate([hi, lo, hi], axis=0)
-        acc[s] += mm(a, jnp.concatenate([ghi, ghi, glo], axis=0), ((0,), (0,)))
-
-    def group(g_, _):
-        for u in range(UNROLL):
-            one(g_ * UNROLL + u)
+        out_ref[rows, :] += mm(a, jnp.concatenate([ghi, ghi, glo], axis=0), ((0,), (0,)))
+
+        @pl.when(i + REST_SLOTS < n)
+        def _():
+            begin(i + REST_SLOTS, 0)
+
         return 0
 
-    def chunk(c, _):
-        tile_copy(tiles_hbm, tiles, sems, c).wait()
-        per = CHUNK // UNROLL
-        return lax.fori_loop(c * per, (c + 1) * per, group, 0)
-
-    lax.fori_loop(0, CHUNKS, chunk, 0)
-    for s in range(SOURCES):
-        out_ref[s * TILE : (s + 1) * TILE, :] = acc[s]
-    kept.wait()
-
-
-def backward_tiles(dest, source, count, g, values, kept):
+    lax.fori_loop(0, n, one, 0)
+
+
+def backward_rest(plan, source, keys, g, values, back):
     return pl.pallas_call(
-        backward_kernel,
-        out_shape=(jax.ShapeDtypeStruct((SOURCES * TILE, WIDTH), F32), jax.ShapeDtypeStruct(kept.shape, F32)),
-        in_specs=[SM, SM, SM, ANY, ANY, ANY],
-        out_specs=(VM, ANY),
+        rest_kernel,
+        out_shape=jax.ShapeDtypeStruct(back.shape, F32),
+        in_specs=[SM, SM, SM, ANY, ANY, VM],
+        out_specs=VM,
         scratch_shapes=[
-            pltpu.VMEM((SLOTS, TILE, TILE), F32),
-            pltpu.VMEM((DESTS, 2 * TILE, TILE), F32),
-            pltpu.VMEM((SOURCES + 1, TILE, WIDTH), F32),
-            DMA((CHUNKS,)),
-            DMA,
-            DMA,
+            pltpu.VMEM((REST_SLOTS, TILE, TILE), F32),
+            pltpu.VMEM((REST_SLOTS, 2 * TILE, TILE), F32),
+            DMA((REST_SLOTS,)),
+            DMA((REST_SLOTS,)),
         ],
         compiler_params=pltpu.CompilerParams(vmem_limit_bytes=VMEM_LIMIT),
-        cost_estimate=pl.CostEstimate(
-            flops=SLOTS * 6 * TILE * TILE * WIDTH, bytes_accessed=22_000_000, transcendentals=0
-        ),
-        name="backward_tiles",
-    )(dest, source, count, g, values, kept)
+        name="backward_rest",
+    )(plan, source, keys, g, values, back)
 
 
 def scatter_kernel(back_ref, part_ref, out_ref, gw_out, near, cross, send_buf, gws, send, recv, ar_send, ar_recv):
@@ -741,18 +830,39 @@
     )(back, part)
 
 
+def finish_kernel(kept, direct, back, gw, kept_out, grad_x, grad_ws, grad_wn, grad_bias):
+    kept_out[...] = kept[...]
+    grad_x[...] = direct[...] + back[...]
+    for i, out in enumerate((grad_ws, grad_wn)):
+        for half in range(2):
+            first = (2 * i + half) * WIDTH
+            out[:, half * TILE : (half + 1) * TILE] = gw[first : first + WIDTH, :]
+    for half in range(2):
+        grad_bias[:, half * TILE : (half + 1) * TILE] = gw[4 * WIDTH + half : 4 * WIDTH + half + 1, :]
+
+
+def finish(kept, direct, back, gw):
+    rows, square = jax.ShapeDtypeStruct(direct.shape, F32), jax.ShapeDtypeStruct((WIDTH, WIDTH), F32)
+    return pl.pallas_call(
+        finish_kernel,
+        out_shape=(rows, rows, square, square, jax.ShapeDtypeStruct((1, WIDTH), F32)),
+        in_specs=[VM] * 4,
+        out_specs=(VM,) * 5,
+        name="finish",
+    )(kept, direct, back, gw)
+
+
 def body(x, ws, wn, bias, tile_values, tile_dest, tile_source, tile_count, cot):
     values = tile_values.reshape(SLOTS, TILE, TILE)
-    dest, source, count = tile_dest.reshape(SLOTS), tile_source.reshape(SLOTS), tile_count.reshape(1)
-    slab = gather_rows(x)
-    part = forward_tiles(dest, source, count, slab, values)
-    layer_out, direct, g, gw_part = exchange(part, x, ws, wn, bias, cot)
-    back, layer_out = backward_tiles(dest, source, count, g, values, layer_out)
+    dest, source = tile_dest.reshape(1, SLOTS), tile_source.reshape(1, SLOTS)
+    count = tile_count.reshape(1)
+    slab, keys = gather_rows(count, dest, source, x)
+    part, plan = forward_tiles(dest, source, keys, count, slab, values)
+    layer_out, direct, g, gw_part, back = exchange(plan, part, x, ws, wn, bias, cot, values)
+    back = backward_rest(plan, source, keys, g, values, back)
     back, gw = scatter_rows(back, gw_part)
-    grad_x = direct + back
-    w = lambda i: jnp.concatenate([gw[i * WIDTH : (i + 1) * WIDTH], gw[(i + 1) * WIDTH : (i + 2) * WIDTH]], axis=1)
-    grad_bias = gw[4 * WIDTH : 4 * WIDTH + 2].reshape(WIDTH)
-    return layer_out, grad_x, w(0), w(2), grad_bias
+    layer_out, grad_x, grad_ws, grad_wn, grad_bias = finish(layer_out, direct, back, gw)
+    return layer_out, grad_x, grad_ws, grad_wn, grad_bias.reshape(WIDTH)
 
 
 def solution(mesh):

time: 172 us -> 161 us (0.936)
  Pallas kernels: 165 us -> 160 us
  other arithmetic: 2.51 us -> 0 us
  local copies, waits for them, and re-layouts: 2.38 us -> 0 us
    pallas_call x3 -> x4, Pallas kernels: 49.5 us -> 37 us  [the longest x1 16.6 us: forward_tiles(): pl.pallas_call(forward_kernel, out_shape=(jax.ShapeDtypeStruct((DESTS, RO...]
    pallas_call x1, Pallas kernels: 96.3 us -> 100 us  [exchange(): pl.pallas_call(exchange_kernel, out_shape=(jax.ShapeDtypeStruct((n, WIDTH...]
    pallas_call x1, Pallas kernels: 19.3 us -> 22.3 us  [scatter_rows(): pl.pallas_call(scatter_kernel, out_shape=(jax.ShapeDtypeStruct((n, WIDTH)...]
where the time goes in v4:
time: 161 us
  Pallas kernels  160 us (99%)
    pallas_call x1, Pallas kernels, exchange(): pl.pallas_call(exchange_kernel, out_shape=(jax.ShapeDtypeStruct((n, WIDTH...  100 us
    pallas_call x1, Pallas kernels, scatter_rows(): pl.pallas_call(scatter_kernel, out_shape=(jax.ShapeDtypeStruct((n, WIDTH)...  22.3 us
    pallas_call x1, Pallas kernels, forward_tiles(): pl.pallas_call(forward_kernel, out_shape=(jax.ShapeDtypeStruct((DESTS, RO...  16.6 us
    pallas_call x1, Pallas kernels, gather_rows(): pl.pallas_call(gather_kernel, out_shape=(jax.ShapeDtypeStruct((4 * x.shap...  15.5 us

profile of v4, /device:TPU:1, one launch (start us, length us, event | category | flops | bytes accessed | tf_op | source)
XLA Modules:
  0.0 160.8 jit_solution(607178769022273328)
XLA Ops:
  1.3 15.5 %gather_rows.1 = (f32[1024,256]{1,0:T(8,128)}, s32[2,192]{1,0:T(2,128)}) custom-call(s32[1]{0:T(128)} %bitcast.8.count, s32[1,192]{1,0:T(1,128)} %bitcast.18, s32[1,192]{1,0:T(1,128)} %bitcast.15, f32[256,256]{1,0:T(8,128)} %x_ref.3), custom_call_target="tpu_custom_call" | custom-call | tf_op jit(solution)/shard_map/gather_rows/pallas_call | solution.py:111
  16.8 16.6 %forward_tiles.1 = (f32[64,264,128]{2,1,0:T(8,128)}, s32[1024]{0:T(1024)}) custom-call(s32[1,192]{1,0:T(1,128)} %bitcast.19, s32[1,192]{1,0:T(1,128)} %bitcast.16, s32[2,192]{1,0:T(2,128)} %get-tuple-element.21.keys, s32[1]{0:T(128)} %bitcast.9.count, f32[1024,256]{1,0:T(8,128)} %get-tuple-element.22.x_ref, f32[192,128,128]{2,1,0:T(8,128)} %bitcast.10), custom_call_target="tpu_custom_call" | custom-call | flops 4831838208 | bytes 22000000 | tf_op jit(solution)/shard_map/forward_tiles/pallas_call | solution.py:210
  33.4 100.3 %exchange.1 = (f32[256,256]{1,0:T(8,128)}, f32[256,256]{1,0:T(8,128)}, f32[4,2,4,2,256,128]{5,4,3,2,1,0:T(8,128)}, f32[40,128]{1,0:T(8,128)}, f32[1024,256]{1,0:T(8,128)}) custom-call(s32[1024]{0:T(1024)} %get-tuple-element.23.plan, f32[4,4,2,2,264,128]{5,4,3,2,1,0:T(8,128)} %bitcast.13, f32[256,256]{1,0:T(8,128)} %x_ref.3, f32[256,256]{1,0:T(8,128)} %ws_ref.1, ...), custom_call_target="tpu_custom_call" | custom-call | tf_op jit(solution)/shard_map/exchange/pallas_call | solution.py:648
  133.7 2.6 %backward_rest.1.back_ref = f32[1024,256]{1,0:T(8,128)} custom-call(s32[1024]{0:T(1024)} %get-tuple-element.23.plan, s32[1,192]{1,0:T(1,128)} %bitcast.17, s32[2,192]{1,0:T(2,128)} %get-tuple-element.21.keys, f32[64,256,128]{2,1,0:T(8,128)} %bitcast.14, f32[192,128,128]{2,1,0:T(8,128)} %bitcast.12, f32[1024,256]{1,0:T(8,128)} %get-tuple-element.28.back_ref), custom_call_target="tpu_custom_call" | custom-call | tf_op jit(solution)/shard_map/backward_rest/pallas_call | solution.py:738
  136.2 22.3 %scatter_rows.1 = (f32[256,256]{1,0:T(8,128)}, f32[1032,128]{1,0:T(8,128)}) custom-call(f32[1024,256]{1,0:T(8,128)} %backward_rest.1.back_ref, f32[40,128]{1,0:T(8,128)} %get-tuple-element.29.part_ref), custom_call_target="tpu_custom_call" | custom-call | tf_op jit(solution)/shard_map/scatter_rows/pallas_call | solution.py:813
  158.6 2.3 %finish.1 = (f32[256,256]{1,0:T(8,128)}, f32[256,256]{1,0:T(8,128)}, f32[256,256]{1,0:T(8,128)}, f32[256,256]{1,0:T(8,128)}, f32[1,256]{1,0:T(1,128)}) custom-call(f32[256,256]{1,0:T(8,128)} %get-tuple-element.25.kept, f32[256,256]{1,0:T(8,128)} %get-tuple-element.26.direct, f32[256,256]{1,0:T(8,128)} %get-tuple-element.30.back, ...), custom_call_target="tpu_custom_call" | custom-call | tf_op jit(solution)/shard_map/finish/pallas_call | solution.py:846

commit v5 on v4

--- a/solution.py
+++ b/solution.py
@@ -28,6 +28,7 @@
 PLAN_SIZE = 1024
 PLAN_VOID = PLAN_SIZE - 1
 REST_SLOTS = 16
+REST_UNROLL = 4
 VMEM_LIMIT = 60 * 1024 * 1024
 
 VM = pl.BlockSpec(memory_space=pltpu.VMEM)
@@ -51,11 +52,14 @@
     return mm(ah, bh, dims) + (mm(ah, bl, dims) + mm(al, bh, dims))
 
 
-def enter(devices):
+def greet(devices):
     barrier = pltpu.get_barrier_semaphore()
     for device in devices:
         pl.semaphore_signal(barrier, inc=1, device_id=device, device_id_type=MESH)
-    pl.semaphore_wait(barrier, len(devices))
+
+
+def enter(devices):
+    pl.semaphore_wait(pltpu.get_barrier_semaphore(), len(devices))
 
 
 def remote(src, dst, send, recv, device):
@@ -80,7 +84,9 @@
     hi, core = lax.div(row, 2), lax.rem(row, 2)
     mate = hi * 2 + (1 - core)
     far = (1 - hi) * 2 + core
-    enter([(mate, col), (far, col)])
+    peers = [(mate, col), (far, col)]
+    greet(peers)
+    enter(peers)
     n = x_ref.shape[0]
     m = n // PIECES
     at = lambda r, c: out_ref.at[pl.ds(pl.multiple_of(r * n + c * m, m), m)]
@@ -398,12 +404,14 @@
         return remote(src, zlast.at[order, rows], zs_send.at[8 + order], zs_recv.at[8 + order], z_mate)
 
     turn = [(2, 1), (1, 1), (3, 1), (2, 0), (0, 1), (1, 0), (3, 0), (0, 0)]
+    peers = [core_mate] + x_others + y_others + z_others
+    greet(peers)
     for which, mine in turn:
         for order in range(2):
             load(order, which, mine).start()
     tile_load = pltpu.make_async_copy(tiles_hbm, tiles, tile_sem)
     tile_load.start()
-    enter([core_mate] + x_others + y_others + z_others)
+    enter(peers)
     for which in (2, 1, 3, 0):
         for order in range(2):
             z_first(order, which).start()
@@ -529,21 +537,20 @@
     gn = dot3(neighbour, grad_pre, ((0,), (0,)))
     flat = [gs[:, 0:TILE], gs[:, TILE:], gn[:, 0:TILE], gn[:, TILE:]]
     gb = jnp.sum(grad_pre, axis=0, keepdims=True)
-    gwp[...] = jnp.zeros_like(gwp)
-    for i, f in enumerate(flat):
-        gwp[i * WIDTH : (i + 1) * WIDTH, :] = f
-    gwp[4 * WIDTH : 4 * WIDTH + 1, :] = gb[:, 0:TILE]
-    gwp[4 * WIDTH + 1 : 4 * WIDTH + 2, :] = gb[:, TILE:]
-
-    n_core, n_x, n_y = 16 * PART_ROWS, 4 * PART_ROWS, PART_ROWS
-    rows_at = lambda c, xx, yy, n: pl.ds(pl.multiple_of((c * 16 + xx * 4 + yy) * PART_ROWS, 8), n)
-    span = lambda *at: gwp.at[rows_at(*at)]
+    blank = jnp.zeros((PARTS * PART_ROWS - 4 * WIDTH - 2, TILE), F32)
+    gwp[...] = jnp.concatenate(flat + [gb[:, 0:TILE], gb[:, TILE:], blank], axis=0).reshape(gwp.shape)
+
     hop = lambda i, src, dst, device: remote(src, dst, ar_send.at[i], ar_recv.at[i], device)
-
-    c1 = [hop(0, span(1 - core, 0, 0, n_core), r1, core_mate)]
-    c2 = [hop(d, span(core, ahead(x, d), 0, n_x), r2.at[d - 1], x_others[d - 1]) for d in range(1, 4)]
-    c3 = [hop(3 + d, span(core, x, ahead(y, d), n_y), r3.at[d - 1], y_others[d - 1]) for d in range(1, 4)]
-    c4 = [hop(7 + d, own_part, r4.at[d], z_others[d]) for d in range(3)]
+    zg = zh * 2 + z
+    c1 = [hop(0, gwp.at[1 - core], r1, core_mate)]
+    z_ring = []
+    for d in range(1, 4):
+        to = ahead(zg, d)
+        z_ring.append((lax.div(to, 2) * 2 + core, column(x, y, lax.rem(to, 2))))
+    c2 = [hop(d, gwp.at[core, :, ahead(zg, d)], r2.at[d - 1], z_ring[d - 1]) for d in range(1, 4)]
+    c3 = [hop(3 + d, gwp.at[core, ahead(x, d), zg], r3.at[d - 1], x_others[d - 1]) for d in range(1, 4)]
+    c4 = [hop(6 + d, own_part, r4.at[y], y_others[d - 1]) for d in range(1, 4)]
+    c4_come = [hop(6 + d, own_part, r4.at[ahead(y, 4 - d)], y_others[d - 1]) for d in range(1, 4)]
 
     def launch(copies):
         for c in copies:
@@ -553,30 +560,28 @@
         for c in copies:
             c.wait()
 
-    def add_parts(at, terms):
-        v = gwp[at, :]
-        for term in terms:
-            v = v + term
-        gwp[at, :] = v
-
     def phase1():
         land(c1)
-        add_parts(rows_at(core, 0, 0, n_core), [r1[...]])
+        gwp[core] += r1[...]
         launch(c2)
 
     def phase2():
         land(c2)
-        add_parts(rows_at(core, x, 0, n_x), [r2[d] for d in range(3)])
+        gwp[core, :, zg] += (r2[0] + r2[1]) + r2[2]
         launch(c3)
 
     def phase3():
         land(c3)
-        own_part[...] = gwp[rows_at(core, x, y, n_y), :] + r3[0] + r3[1] + r3[2]
+        own_part[...] = gwp[core, x, zg] + r3[0] + r3[1] + r3[2]
         launch(c4)
 
     def phase4():
-        land(c4)
-        gw_out[...] = (own_part[...] + r4[0]) + (r4[1] + r4[2])
+        for c in c4_come:
+            c.wait_recv()
+        for c in c4:
+            c.wait_send()
+        terms = [jnp.where(y == i, own_part[...], r4[i]) for i in range(4)]
+        gw_out[...] = (terms[0] + terms[1]) + (terms[2] + terms[3])
 
     launch(c1)
     direct_out[...] = dot3(grad_pre, ws, ((1,), (1,)))
@@ -665,11 +670,11 @@
             *[pltpu.VMEM((2, 4, 2, 2 * TILE, TILE), F32) for _ in range(4)],
             pltpu.VMEM((SLOTS, TILE, TILE), F32),
             pltpu.VMEM((n, WIDTH), F32),
-            pltpu.VMEM((PARTS * PART_ROWS, TILE), F32),
-            pltpu.VMEM((16 * PART_ROWS, TILE), F32),
-            pltpu.VMEM((3, 4 * PART_ROWS, TILE), F32),
+            pltpu.VMEM((2, 4, 4, PART_ROWS, TILE), F32),
+            pltpu.VMEM((4, 4, PART_ROWS, TILE), F32),
+            pltpu.VMEM((3, 4, PART_ROWS, TILE), F32),
             pltpu.VMEM((3, PART_ROWS, TILE), F32),
-            pltpu.VMEM((3, PART_ROWS, TILE), F32),
+            pltpu.VMEM((4, PART_ROWS, TILE), F32),
             pltpu.VMEM((PART_ROWS, TILE), F32),
             DMA((16,)),
             DMA((SLICES, 6)),
@@ -715,23 +720,35 @@
     lax.fori_loop(0, jnp.minimum(n, REST_SLOTS), begin, 0)
     out_ref[...] = back_ref[...]
 
-    def one(i, _):
-        for c in copies(i):
-            c.wait()
-        slot = lax.rem(i, REST_SLOTS)
-        rows = pl.ds(pl.multiple_of(source[0, plan[PLAN_LIST + i]] * TILE, TILE), TILE)
-        hi, lo = split(tiles[slot])
-        ghi, glo = split(jnp.concatenate([g[slot, 0:TILE, :], g[slot, TILE:, :]], axis=1))
-        a = jnp.concatenate([hi, lo, hi], axis=0)
-        out_ref[rows, :] += mm(a, jnp.concatenate([ghi, ghi, glo], axis=0), ((0,), (0,)))
-
-        @pl.when(i + REST_SLOTS < n)
-        def _():
-            begin(i + REST_SLOTS, 0)
+    def some(k, _):
+        first = k * REST_UNROLL
+        for u in range(REST_UNROLL):
+
+            @pl.when(first + u < n)
+            def _():
+                for c in copies(first + u):
+                    c.wait()
+
+        products = []
+        for u in range(REST_UNROLL):
+            i = jnp.minimum(first + u, n - 1)
+            slot = lax.rem(i, REST_SLOTS)
+            hi, lo = split(tiles[slot] * jnp.where(first + u < n, 1.0, 0.0))
+            ghi, glo = split(jnp.concatenate([g[slot, 0:TILE, :], g[slot, TILE:, :]], axis=1))
+            a = jnp.concatenate([hi, lo, hi], axis=0)
+            products.append((i, mm(a, jnp.concatenate([ghi, ghi, glo], axis=0), ((0,), (0,)))))
+        for i, p in products:
+            rows = pl.ds(pl.multiple_of(source[0, plan[PLAN_LIST + i]] * TILE, TILE), TILE)
+            out_ref[rows, :] += p
+        for u in range(REST_UNROLL):
+
+            @pl.when(first + u + REST_SLOTS < n)
+            def _():
+                begin(first + u + REST_SLOTS, 0)
 
         return 0
 
-    lax.fori_loop(0, n, one, 0)
+    lax.fori_loop(0, lax.div(n + REST_UNROLL - 1, REST_UNROLL), some, 0)
 
 
 def backward_rest(plan, source, keys, g, values, back):
@@ -751,22 +768,34 @@
     )(plan, source, keys, g, values, back)
 
 
-def scatter_kernel(back_ref, part_ref, out_ref, gw_out, near, cross, send_buf, gws, send, recv, ar_send, ar_recv):
+def scatter_kernel(
+    back_hbm, part_ref, out_hbm, gw_hbm,
+    back_ref, out_ref, near, cross, send_buf, gws, send, recv, ar_send, ar_recv, load_sem, out_sem,
+):
     row, col = lax.axis_index("row"), lax.axis_index("col")
     hi, core = lax.div(row, 2), lax.rem(row, 2)
     x, y, z = lax.div(col, 8), lax.rem(lax.div(col, 2), 4), lax.rem(col, 2)
     column = lambda xx, yy, zz: xx * 8 + yy * 2 + zz
     ahead = lambda p, d: lax.rem(p + d, 4)
     x_others = [(row, column(ahead(x, d), y, z)) for d in range(1, 4)]
-    y_others = [(row, column(x, ahead(y, d), z)) for d in range(1, 4)]
+    zg = hi * 2 + z
+    z_others = []
+    for d in range(1, 4):
+        to = ahead(zg, d)
+        z_others.append((lax.div(to, 2) * 2 + core, column(x, y, lax.rem(to, 2))))
     mate = (hi * 2 + (1 - core), col)
-    far = ((1 - hi) * 2 + core, col)
-    enter([mate, far] + x_others + y_others)
+    far = z_others[1]
+    peers = [mate] + x_others + z_others
+    greet(peers)
+    load = pltpu.make_async_copy(back_hbm, back_ref, load_sem)
+    load.start()
+    enter(peers)
     n = out_ref.shape[0]
     m = n // PIECES
     at = lambda r, c: pl.ds(pl.multiple_of(r * n + c * m, m), m)
     piece = lambda c: pl.ds(c * m, m)
     far_row, far_mate = (1 - hi) * 2 + core, (1 - hi) * 2 + (1 - core)
+    write = lambda c: pltpu.make_async_copy(out_ref.at[piece(c)], out_hbm.at[piece(c)], out_sem.at[c])
     first, second, third = [], [], []
     for c in range(PIECES):
         src = back_ref.at[at(far_mate, c)]
@@ -774,16 +803,15 @@
         src = back_ref.at[at(hi * 2 + (1 - core), c)]
         second.append(remote(src, near.at[1, piece(c)], send.at[1, c], recv.at[1, c], mate))
         third.append(remote(send_buf.at[piece(c)], cross.at[piece(c)], send.at[2, c], recv.at[2, c], far))
+    load.wait()
     for c in first + second:
         c.start()
 
-    rows_at = lambda c, xx, yy, k: pl.ds(pl.multiple_of((c * 16 + xx * 4 + yy) * PART_ROWS, 8), k)
-    summed = lambda *w: gws.at[rows_at(*w)]
     hop = lambda i, ref, device: remote(ref, ref, ar_send.at[i], ar_recv.at[i], device)
-    gws[rows_at(core, x, y, PART_ROWS), :] = part_ref[...]
-    c5 = [hop(d, summed(core, x, y, PART_ROWS), y_others[d]) for d in range(3)]
-    c6 = [hop(3 + d, summed(core, x, 0, 4 * PART_ROWS), x_others[d]) for d in range(3)]
-    c7 = [hop(6, summed(core, 0, 0, 16 * PART_ROWS), mate)]
+    gws[core, x, zg] = part_ref[...]
+    c5 = [hop(d, gws.at[core, x, zg], z_others[d]) for d in range(3)]
+    c6 = [hop(3 + d, gws.at[core, x], x_others[d]) for d in range(3)]
+    c7 = [hop(6, gws.at[core], mate)]
     for c in c5:
         c.start()
     for c in range(PIECES):
@@ -791,43 +819,54 @@
         send_buf[piece(c), :] = back_ref[at(far_row, c), :] + near[0, piece(c), :]
         third[c].start()
     for d in range(3):
-        hop(d, summed(core, x, ahead(y, 3 - d), PART_ROWS), y_others[d]).wait_recv()
+        hop(d, gws.at[core, x, ahead(zg, 3 - d)], z_others[d]).wait_recv()
     for c in c6:
         c.start()
     for d in range(3):
-        hop(3 + d, summed(core, ahead(x, 3 - d), 0, 4 * PART_ROWS), x_others[d]).wait_recv()
+        hop(3 + d, gws.at[core, ahead(x, 3 - d)], x_others[d]).wait_recv()
     for c in c7:
         c.start()
     for c in range(PIECES):
         second[c].wait_recv()
         third[c].wait_recv()
         out_ref[piece(c), :] = back_ref[at(row, c), :] + near[1, piece(c), :] + cross[piece(c), :]
-    hop(6, summed(1 - core, 0, 0, 16 * PART_ROWS), mate).wait_recv()
-    gw_out[...] = gws[0 : 4 * WIDTH + 8, :]
+        write(c).start()
+    hop(6, gws.at[1 - core], mate).wait_recv()
+    gw_write = pltpu.make_async_copy(gws, gw_hbm, out_sem.at[PIECES])
+    gw_write.start()
+    for c in range(PIECES):
+        write(c).wait()
+    gw_write.wait()
     for c in first + second + third + c5 + c6 + c7:
         c.wait_send()
 
 
 def scatter_rows(back, part):
     n = back.shape[0] // 4
-    return pl.pallas_call(
+    parts = (2, 4, 4, PART_ROWS, TILE)
+    back, gw = pl.pallas_call(
         scatter_kernel,
-        out_shape=(jax.ShapeDtypeStruct((n, WIDTH), F32), jax.ShapeDtypeStruct((4 * WIDTH + 8, TILE), F32)),
-        in_specs=[VM, VM],
-        out_specs=(VM, VM),
+        out_shape=(jax.ShapeDtypeStruct((n, WIDTH), F32), jax.ShapeDtypeStruct(parts, F32)),
+        in_specs=[ANY, VM],
+        out_specs=(ANY, ANY),
         scratch_shapes=[
+            pltpu.VMEM(back.shape, F32),
+            pltpu.VMEM((n, WIDTH), F32),
             pltpu.VMEM((2, n, WIDTH), F32),
             pltpu.VMEM((n, WIDTH), F32),
             pltpu.VMEM((n, WIDTH), F32),
-            pltpu.VMEM((PARTS * PART_ROWS, TILE), F32),
+            pltpu.VMEM(parts, F32),
             DMA((3, PIECES)),
             DMA((3, PIECES)),
             DMA((7,)),
             DMA((7,)),
+            DMA,
+            DMA((PIECES + 1,)),
         ],
         compiler_params=pltpu.CompilerParams(collective_id=2, has_side_effects=True),
         name="scatter_rows",
     )(back, part)
+    return back, gw.reshape(PARTS * PART_ROWS, TILE)
 
 
 def finish_kernel(kept, direct, back, gw, kept_out, grad_x, grad_ws, grad_wn, grad_bias):

time: 161 us -> 160 us (level)
  the two profiles are of different devices: /device:TPU:1 before, /device:TPU:9 now
where the time goes in v5:
time: 160 us
  Pallas kernels  158 us (99%)
    pallas_call x1, Pallas kernels, exchange(): pl.pallas_call(exchange_kernel, out_shape=(jax.ShapeDtypeStruct((n, WIDTH...  96.2 us
    pallas_call x1, Pallas kernels, scatter_rows(): pl.pallas_call(scatter_kernel, out_shape=(jax.ShapeDtypeStruct((n, WIDTH)...  26.1 us
    pallas_call x1, Pallas kernels, forward_tiles(): pl.pallas_call(forward_kernel, out_shape=(jax.ShapeDtypeStruct((DESTS, RO...  16.6 us
    pallas_call x1, Pallas kernels, gather_rows(): pl.pallas_call(gather_kernel, out_shape=(jax.ShapeDtypeStruct((4 * x.shap...  14.6 us

profile of v5, /device:TPU:9, one launch (start us, length us, event | category | flops | bytes accessed | tf_op | source)
XLA Modules:
  0.0 159.7 jit_solution(244951684629839973)
XLA Ops:
  1.3 14.6 %gather_rows.1 = (f32[1024,256]{1,0:T(8,128)}, s32[2,192]{1,0:T(2,128)}) custom-call(s32[1]{0:T(128)} %bitcast.9.count, s32[1,192]{1,0:T(1,128)} %bitcast.20, s32[1,192]{1,0:T(1,128)} %bitcast.17, f32[256,256]{1,0:T(8,128)} %x_ref.3), custom_call_target="tpu_custom_call" | custom-call | tf_op jit(solution)/shard_map/gather_rows/pallas_call | solution.py:117
  15.9 16.6 %forward_tiles.1 = (f32[64,264,128]{2,1,0:T(8,128)}, s32[1024]{0:T(1024)}) custom-call(s32[1,192]{1,0:T(1,128)} %bitcast.21, s32[1,192]{1,0:T(1,128)} %bitcast.18, s32[2,192]{1,0:T(2,128)} %get-tuple-element.21.keys, s32[1]{0:T(128)} %bitcast.10.count, f32[1024,256]{1,0:T(8,128)} %get-tuple-element.22.x_ref, f32[192,128,128]{2,1,0:T(8,128)} %bitcast.11), custom_call_target="tpu_custom_call" | custom-call | flops 4831838208 | bytes 22000000 | tf_op jit(solution)/shard_map/forward_tiles/pallas_call | solution.py:216
  32.5 96.2 %exchange.1 = (f32[256,256]{1,0:T(8,128)}, f32[256,256]{1,0:T(8,128)}, f32[4,2,4,2,256,128]{5,4,3,2,1,0:T(8,128)}, f32[40,128]{1,0:T(8,128)}, f32[1024,256]{1,0:T(8,128)}) custom-call(s32[1024]{0:T(1024)} %get-tuple-element.23.plan, f32[4,4,2,2,264,128]{5,4,3,2,1,0:T(8,128)} %bitcast.14, f32[256,256]{1,0:T(8,128)} %x_ref.3, f32[256,256]{1,0:T(8,128)} %ws_ref.1, ...), custom_call_target="tpu_custom_call" | custom-call | tf_op jit(solution)/shard_map/exchange/pallas_call | solution.py:653
  128.7 2.6 %backward_rest.1.back_hbm = f32[1024,256]{1,0:T(8,128)} custom-call(s32[1024]{0:T(1024)} %get-tuple-element.23.plan, s32[1,192]{1,0:T(1,128)} %bitcast.19, s32[2,192]{1,0:T(2,128)} %get-tuple-element.21.keys, f32[64,256,128]{2,1,0:T(8,128)} %bitcast.15, f32[192,128,128]{2,1,0:T(8,128)} %bitcast.13, f32[1024,256]{1,0:T(8,128)} %get-tuple-element.28.back_ref), custom_call_target="tpu_custom_call" | custom-call | tf_op jit(solution)/shard_map/backward_rest/pallas_call | solution.py:755
  131.3 26.1 %scatter_rows.1 = (f32[256,256]{1,0:T(8,128)}, f32[2,4,4,40,128]{4,3,2,1,0:T(8,128)}) custom-call(f32[1024,256]{1,0:T(8,128)} %backward_rest.1.back_hbm, f32[40,128]{1,0:T(8,128)} %get-tuple-element.29.part_ref), custom_call_target="tpu_custom_call" | custom-call | tf_op jit(solution)/shard_map/scatter_rows/pallas_call | solution.py:847
  157.4 2.3 %finish.1 = (f32[256,256]{1,0:T(8,128)}, f32[256,256]{1,0:T(8,128)}, f32[256,256]{1,0:T(8,128)}, f32[256,256]{1,0:T(8,128)}, f32[1,256]{1,0:T(1,128)}) custom-call(f32[256,256]{1,0:T(8,128)} %get-tuple-element.25.kept, f32[256,256]{1,0:T(8,128)} %get-tuple-element.26.direct, f32[256,256]{1,0:T(8,128)} %get-tuple-element.30.back, f32[1280,128]{1,0:T(8,128)} %bitcast.16), custom_call_target="tpu_custom_call" | custom-call | tf_op jit(solution)/shard_map/finish/pallas_call | solution.py:885

commit v6 on v5

--- a/solution.py
+++ b/solution.py
@@ -306,7 +306,11 @@
                 )
             ):
                 src = acc.at[(*self.blk(j), pl.ds(*rows))]
-                self.copies.append(remote(src, to, rs_send.at[self.n, i], rs_recv.at[self.n, i], device))
+                self.copies.append(remote(src, to, rs_send.at[self.n], rs_recv.at[self.n, min(i, 2)], device))
+            rows = pl.ds(self.top[0], self.top[1] + self.low[1])
+            come, gone = arrivals.at[self.n, :, rows], acc.at[0, pl.ds(0, 3), 0, 0, rows]
+            self.come = remote(come, come, rs_send.at[self.n], rs_recv.at[self.n, 2], up)
+            self.gone = remote(gone, gone, rs_send.at[self.n], rs_recv.at[self.n, 2], up)
 
         def issue(self):
             for c in self.copies[:4]:
@@ -320,15 +324,13 @@
                 self.copies[4 + i].start()
 
         def finish(self):
-            for c in self.copies[2:]:
-                c.wait_recv()
+            self.come.wait_recv()
             rows = pl.ds(self.top[0], self.top[1] + self.low[1])
             at = (*self.blk(0), rows, slice(None))
             acc[at] += arrivals[self.n, 0, rows, :] + arrivals[self.n, 1, rows, :]
 
         def drain(self):
-            for c in self.copies:
-                c.wait_send()
+            self.gone.wait_send()
 
     def quarter_of(which, mine):
         return mine * 2 + which // 2, (which & 1) ^ (which // 2)
@@ -360,8 +362,15 @@
             ):
                 src, come = blk(leaves).at[pl.ds(*rows)], blk(comes).at[pl.ds(*rows)]
                 dst = src if w == 0 else come
-                self.out.append(remote(src, dst, ag_send.at[n, i], ag_recv.at[n, i], device))
-                self.come.append(remote(come, come, ag_send.at[n, i], ag_recv.at[n, i], device))
+                kind = i if i < 2 else i // 2 + 1
+                self.out.append(remote(src, dst, ag_send.at[n], ag_recv.at[n, kind], device))
+                if i < 2:
+                    self.come.append(remote(come, come, ag_send.at[n], ag_recv.at[n, kind], device))
+            rows = pl.ds(top[0], top[1] + low[1])
+            one, three = g0.at[0, 0, 0, rows], g0.at[0, pl.ds(0, 3), 0, rows]
+            self.beside = remote(one, one, ag_send.at[n], ag_recv.at[n, 2], up)
+            self.across = remote(blk(2).at[rows], blk(2).at[rows], ag_send.at[n], ag_recv.at[n, 3], up)
+            self.gone = remote(three, three, ag_send.at[n], ag_recv.at[n, 3], up)
 
         def issue(self):
             for c in self.out[:4]:
@@ -373,16 +382,13 @@
                 self.out[4 + i].start()
 
         def near(self):
-            for c in self.come[2:4]:
-                c.wait_recv()
+            self.beside.wait_recv()
 
         def finish(self):
-            for c in self.come[4:]:
-                c.wait_recv()
+            self.across.wait_recv()
 
         def drain(self):
-            for c in self.out:
-                c.wait_send()
+            self.gone.wait_send()
 
     def strip(ref, order, which, mine, rows=None):
         q = ahead(y if order == 0 else x, which)
@@ -677,12 +683,12 @@
             pltpu.VMEM((4, PART_ROWS, TILE), F32),
             pltpu.VMEM((PART_ROWS, TILE), F32),
             DMA((16,)),
-            DMA((SLICES, 6)),
-            DMA((SLICES, 6)),
+            DMA((SLICES,)),
+            DMA((SLICES, 3)),
             DMA((10,)),
             DMA((10,)),
-            DMA((SLICES, 6)),
-            DMA((SLICES, 6)),
+            DMA((SLICES,)),
+            DMA((SLICES, 4)),
             DMA((10,)),
             DMA((10,)),
             DMA((AR_SENDS,)),

time: 160 us -> 158 us (0.988)
  the two profiles are of different devices: /device:TPU:9 before, /device:TPU:1 now
where the time goes in v6:
time: 158 us; the launch traced here: 157 us
  Pallas kernels  156 us (99%)
    pallas_call x1, Pallas kernels, exchange(): pl.pallas_call(exchange_kernel, out_shape=(jax.ShapeDtypeStruct((n, WIDTH...  94.7 us
    pallas_call x1, Pallas kernels, scatter_rows(): pl.pallas_call(scatter_kernel, out_shape=(jax.ShapeDtypeStruct((n, WIDTH)...  22.5 us
    pallas_call x1, Pallas kernels, forward_tiles(): pl.pallas_call(forward_kernel, out_shape=(jax.ShapeDtypeStruct((DESTS, RO...  16.7 us
    pallas_call x1, Pallas kernels, gather_rows(): pl.pallas_call(gather_kernel, out_shape=(jax.ShapeDtypeStruct((4 * x.shap...  15.5 us
    pallas_call x1, Pallas kernels, backward_rest(): pl.pallas_call(rest_kernel, out_shape=jax.ShapeDtypeStruct(back.shape, F3...  4.44 us

profile of v6, /device:TPU:1, one launch (start us, length us, event | category | flops | bytes accessed | tf_op | source)
XLA Modules:
  0.0 157.5 jit_solution(6033119803008233470)
XLA Ops:
  1.3 15.5 %gather_rows.1 = (f32[1024,256]{1,0:T(8,128)}, s32[2,192]{1,0:T(2,128)}) custom-call(s32[1]{0:T(128)} %bitcast.9.count, s32[1,192]{1,0:T(1,128)} %bitcast.20, s32[1,192]{1,0:T(1,128)} %bitcast.17, f32[256,256]{1,0:T(8,128)} %x_ref.3), custom_call_target="tpu_custom_call" | custom-call | tf_op jit(solution)/shard_map/gather_rows/pallas_call | solution.py:117
  16.8 16.7 %forward_tiles.1 = (f32[64,264,128]{2,1,0:T(8,128)}, s32[1024]{0:T(1024)}) custom-call(s32[1,192]{1,0:T(1,128)} %bitcast.21, s32[1,192]{1,0:T(1,128)} %bitcast.18, s32[2,192]{1,0:T(2,128)} %get-tuple-element.21.keys, s32[1]{0:T(128)} %bitcast.10.count, f32[1024,256]{1,0:T(8,128)} %get-tuple-element.22.x_ref, f32[192,128,128]{2,1,0:T(8,128)} %bitcast.11), custom_call_target="tpu_custom_call" | custom-call | flops 4831838208 | bytes 22000000 | tf_op jit(solution)/shard_map/forward_tiles/pallas_call | solution.py:216
  33.4 94.7 %exchange.1 = (f32[256,256]{1,0:T(8,128)}, f32[256,256]{1,0:T(8,128)}, f32[4,2,4,2,256,128]{5,4,3,2,1,0:T(8,128)}, f32[40,128]{1,0:T(8,128)}, f32[1024,256]{1,0:T(8,128)}) custom-call(s32[1024]{0:T(1024)} %get-tuple-element.23.plan, f32[4,4,2,2,264,128]{5,4,3,2,1,0:T(8,128)} %bitcast.14, f32[256,256]{1,0:T(8,128)} %x_ref.3, f32[256,256]{1,0:T(8,128)} %ws_ref.1, ...), custom_call_target="tpu_custom_call" | custom-call | tf_op jit(solution)/shard_map/exchange/pallas_call | solution.py:659
  128.2 4.4 %backward_rest.1.back_hbm = f32[1024,256]{1,0:T(8,128)} custom-call(s32[1024]{0:T(1024)} %get-tuple-element.23.plan, s32[1,192]{1,0:T(1,128)} %bitcast.19, s32[2,192]{1,0:T(2,128)} %get-tuple-element.21.keys, f32[64,256,128]{2,1,0:T(8,128)} %bitcast.15, f32[192,128,128]{2,1,0:T(8,128)} %bitcast.13, f32[1024,256]{1,0:T(8,128)} %get-tuple-element.28.back_ref), custom_call_target="tpu_custom_call" | custom-call | tf_op jit(solution)/shard_map/backward_rest/pallas_call | solution.py:761
  132.6 22.5 %scatter_rows.1 = (f32[256,256]{1,0:T(8,128)}, f32[2,4,4,40,128]{4,3,2,1,0:T(8,128)}) custom-call(f32[1024,256]{1,0:T(8,128)} %backward_rest.1.back_hbm, f32[40,128]{1,0:T(8,128)} %get-tuple-element.29.part_ref), custom_call_target="tpu_custom_call" | custom-call | tf_op jit(solution)/shard_map/scatter_rows/pallas_call | solution.py:853
  155.1 2.3 %finish.1 = (f32[256,256]{1,0:T(8,128)}, f32[256,256]{1,0:T(8,128)}, f32[256,256]{1,0:T(8,128)}, f32[256,256]{1,0:T(8,128)}, f32[1,256]{1,0:T(1,128)}) custom-call(f32[256,256]{1,0:T(8,128)} %get-tuple-element.25.kept, f32[256,256]{1,0:T(8,128)} %get-tuple-element.26.direct, f32[256,256]{1,0:T(8,128)} %get-tuple-element.30.back, f32[1280,128]{1,0:T(8,128)} %bitcast.16), custom_call_target="tpu_custom_call" | custom-call | tf_op jit(solution)/shard_map/finish/pallas_call | solution.py:891

commit v7 on v6

--- a/solution.py
+++ b/solution.py
@@ -553,8 +553,8 @@
     for d in range(1, 4):
         to = ahead(zg, d)
         z_ring.append((lax.div(to, 2) * 2 + core, column(x, y, lax.rem(to, 2))))
-    c2 = [hop(d, gwp.at[core, :, ahead(zg, d)], r2.at[d - 1], z_ring[d - 1]) for d in range(1, 4)]
-    c3 = [hop(3 + d, gwp.at[core, ahead(x, d), zg], r3.at[d - 1], x_others[d - 1]) for d in range(1, 4)]
+    c2 = [hop(d, gwp.at[core, ahead(zg, d)], r2.at[d - 1], z_ring[d - 1]) for d in range(1, 4)]
+    c3 = [hop(3 + d, gwp.at[core, zg, ahead(x, d)], r3.at[d - 1], x_others[d - 1]) for d in range(1, 4)]
     c4 = [hop(6 + d, own_part, r4.at[y], y_others[d - 1]) for d in range(1, 4)]
     c4_come = [hop(6 + d, own_part, r4.at[ahead(y, 4 - d)], y_others[d - 1]) for d in range(1, 4)]
 
@@ -573,12 +573,12 @@
 
     def phase2():
         land(c2)
-        gwp[core, :, zg] += (r2[0] + r2[1]) + r2[2]
+        gwp[core, zg] += (r2[0] + r2[1]) + r2[2]
         launch(c3)
 
     def phase3():
         land(c3)
-        own_part[...] = gwp[core, x, zg] + r3[0] + r3[1] + r3[2]
+        own_part[...] = gwp[core, zg, x] + r3[0] + r3[1] + r3[2]
         launch(c4)
 
     def phase4():
@@ -814,9 +814,9 @@
         c.start()
 
     hop = lambda i, ref, device: remote(ref, ref, ar_send.at[i], ar_recv.at[i], device)
-    gws[core, x, zg] = part_ref[...]
-    c5 = [hop(d, gws.at[core, x, zg], z_others[d]) for d in range(3)]
-    c6 = [hop(3 + d, gws.at[core, x], x_others[d]) for d in range(3)]
+    gws[core, zg, x] = part_ref[...]
+    c5 = [hop(d, gws.at[core, zg, x], x_others[d]) for d in range(3)]
+    c6 = [hop(3 + d, gws.at[core, zg], z_others[d]) for d in range(3)]
     c7 = [hop(6, gws.at[core], mate)]
     for c in c5:
         c.start()
@@ -825,11 +825,11 @@
         send_buf[piece(c), :] = back_ref[at(far_row, c), :] + near[0, piece(c), :]
         third[c].start()
     for d in range(3):
-        hop(d, gws.at[core, x, ahead(zg, 3 - d)], z_others[d]).wait_recv()
+        hop(d, gws.at[core, zg, ahead(x, 3 - d)], x_others[d]).wait_recv()
     for c in c6:
         c.start()
     for d in range(3):
-        hop(3 + d, gws.at[core, ahead(x, 3 - d)], x_others[d]).wait_recv()
+        hop(3 + d, gws.at[core, ahead(zg, 3 - d)], z_others[d]).wait_recv()
     for c in c7:
         c.start()
     for c in range(PIECES):

time: 158 us -> 156 us (0.987)
    pallas_call x1, Pallas kernels: 4.44 us -> 2.57 us  [backward_rest(): pl.pallas_call(rest_kernel, out_shape=jax.ShapeDtypeStruct(back.shape, F3...]
where the time goes in v7:
time: 156 us; the launch traced here: 157 us
  Pallas kernels  156 us (100%)
    pallas_call x1, Pallas kernels, exchange(): pl.pallas_call(exchange_kernel, out_shape=(jax.ShapeDtypeStruct((n, WIDTH...  94.6 us
    pallas_call x1, Pallas kernels, scatter_rows(): pl.pallas_call(scatter_kernel, out_shape=(jax.ShapeDtypeStruct((n, WIDTH)...  24 us
    pallas_call x1, Pallas kernels, forward_tiles(): pl.pallas_call(forward_kernel, out_shape=(jax.ShapeDtypeStruct((DESTS, RO...  16.6 us
    pallas_call x1, Pallas kernels, gather_rows(): pl.pallas_call(gather_kernel, out_shape=(jax.ShapeDtypeStruct((4 * x.shap...  15.5 us

profile of v7, /device:TPU:1, one launch (start us, length us, event | category | flops | bytes accessed | tf_op | source)
XLA Modules:
  0.0 156.9 jit_solution(16625135943184033599)
XLA Ops:
  1.3 15.5 %gather_rows.1 = (f32[1024,256]{1,0:T(8,128)}, s32[2,192]{1,0:T(2,128)}) custom-call(s32[1]{0:T(128)} %bitcast.9.count, s32[1,192]{1,0:T(1,128)} %bitcast.20, s32[1,192]{1,0:T(1,128)} %bitcast.17, f32[256,256]{1,0:T(8,128)} %x_ref.3), custom_call_target="tpu_custom_call" | custom-call | tf_op jit(solution)/shard_map/gather_rows/pallas_call | solution.py:117
  16.8 16.6 %forward_tiles.1 = (f32[64,264,128]{2,1,0:T(8,128)}, s32[1024]{0:T(1024)}) custom-call(s32[1,192]{1,0:T(1,128)} %bitcast.21, s32[1,192]{1,0:T(1,128)} %bitcast.18, s32[2,192]{1,0:T(2,128)} %get-tuple-element.21.keys, s32[1]{0:T(128)} %bitcast.10.count, f32[1024,256]{1,0:T(8,128)} %get-tuple-element.22.x_ref, f32[192,128,128]{2,1,0:T(8,128)} %bitcast.11), custom_call_target="tpu_custom_call" | custom-call | flops 4831838208 | bytes 22000000 | tf_op jit(solution)/shard_map/forward_tiles/pallas_call | solution.py:216
  33.4 94.6 %exchange.1 = (f32[256,256]{1,0:T(8,128)}, f32[256,256]{1,0:T(8,128)}, f32[4,2,4,2,256,128]{5,4,3,2,1,0:T(8,128)}, f32[40,128]{1,0:T(8,128)}, f32[1024,256]{1,0:T(8,128)}) custom-call(s32[1024]{0:T(1024)} %get-tuple-element.23.plan, f32[4,4,2,2,264,128]{5,4,3,2,1,0:T(8,128)} %bitcast.14, f32[256,256]{1,0:T(8,128)} %x_ref.3, f32[256,256]{1,0:T(8,128)} %ws_ref.1, ...), custom_call_target="tpu_custom_call" | custom-call | tf_op jit(solution)/shard_map/exchange/pallas_call | solution.py:659
  127.9 2.6 %backward_rest.1.back_hbm = f32[1024,256]{1,0:T(8,128)} custom-call(s32[1024]{0:T(1024)} %get-tuple-element.23.plan, s32[1,192]{1,0:T(1,128)} %bitcast.19, s32[2,192]{1,0:T(2,128)} %get-tuple-element.21.keys, f32[64,256,128]{2,1,0:T(8,128)} %bitcast.15, f32[192,128,128]{2,1,0:T(8,128)} %bitcast.13, f32[1024,256]{1,0:T(8,128)} %get-tuple-element.28.back_ref), custom_call_target="tpu_custom_call" | custom-call | tf_op jit(solution)/shard_map/backward_rest/pallas_call | solution.py:761
  130.5 24.0 %scatter_rows.1 = (f32[256,256]{1,0:T(8,128)}, f32[2,4,4,40,128]{4,3,2,1,0:T(8,128)}) custom-call(f32[1024,256]{1,0:T(8,128)} %backward_rest.1.back_hbm, f32[40,128]{1,0:T(8,128)} %get-tuple-element.29.part_ref), custom_call_target="tpu_custom_call" | custom-call | tf_op jit(solution)/shard_map/scatter_rows/pallas_call | solution.py:853
  154.6 2.3 %finish.1 = (f32[256,256]{1,0:T(8,128)}, f32[256,256]{1,0:T(8,128)}, f32[256,256]{1,0:T(8,128)}, f32[256,256]{1,0:T(8,128)}, f32[1,256]{1,0:T(1,128)}) custom-call(f32[256,256]{1,0:T(8,128)} %get-tuple-element.25.kept, f32[256,256]{1,0:T(8,128)} %get-tuple-element.26.direct, f32[256,256]{1,0:T(8,128)} %get-tuple-element.30.back, f32[1280,128]{1,0:T(8,128)} %bitcast.16), custom_call_target="tpu_custom_call" | custom-call | tf_op jit(solution)/shard_map/finish/pallas_call | solution.py:891

commit v8 on v7

--- a/solution.py
+++ b/solution.py
@@ -809,16 +809,15 @@
         src = back_ref.at[at(hi * 2 + (1 - core), c)]
         second.append(remote(src, near.at[1, piece(c)], send.at[1, c], recv.at[1, c], mate))
         third.append(remote(send_buf.at[piece(c)], cross.at[piece(c)], send.at[2, c], recv.at[2, c], far))
-    load.wait()
-    for c in first + second:
-        c.start()
-
     hop = lambda i, ref, device: remote(ref, ref, ar_send.at[i], ar_recv.at[i], device)
     gws[core, zg, x] = part_ref[...]
     c5 = [hop(d, gws.at[core, zg, x], x_others[d]) for d in range(3)]
     c6 = [hop(3 + d, gws.at[core, zg], z_others[d]) for d in range(3)]
     c7 = [hop(6, gws.at[core], mate)]
     for c in c5:
+        c.start()
+    load.wait()
+    for c in first + second:
         c.start()
     for c in range(PIECES):
         first[c].wait_recv()

time: 156 us -> 156 us (level); the launches traced: 157 us -> 155 us
  Pallas kernels: 156 us -> 154 us
    pallas_call x1, Pallas kernels: 24 us -> 22.1 us  [scatter_rows(): pl.pallas_call(scatter_kernel, out_shape=(jax.ShapeDtypeStruct((n, WIDTH)...]
where the time goes in v8:
time: 156 us; the launch traced here: 155 us
  Pallas kernels  154 us (99%)
    pallas_call x1, Pallas kernels, exchange(): pl.pallas_call(exchange_kernel, out_shape=(jax.ShapeDtypeStruct((n, WIDTH...  94.7 us
    pallas_call x1, Pallas kernels, scatter_rows(): pl.pallas_call(scatter_kernel, out_shape=(jax.ShapeDtypeStruct((n, WIDTH)...  22.1 us
    pallas_call x1, Pallas kernels, forward_tiles(): pl.pallas_call(forward_kernel, out_shape=(jax.ShapeDtypeStruct((DESTS, RO...  16.6 us
    pallas_call x1, Pallas kernels, gather_rows(): pl.pallas_call(gather_kernel, out_shape=(jax.ShapeDtypeStruct((4 * x.shap...  15.5 us

profile of v8, /device:TPU:1, one launch (start us, length us, event | category | flops | bytes accessed | tf_op | source)
XLA Modules:
  0.0 155.1 jit_solution(16489519534082850004)
XLA Ops:
  1.3 15.5 %gather_rows.1 = (f32[1024,256]{1,0:T(8,128)}, s32[2,192]{1,0:T(2,128)}) custom-call(s32[1]{0:T(128)} %bitcast.9.count, s32[1,192]{1,0:T(1,128)} %bitcast.20, s32[1,192]{1,0:T(1,128)} %bitcast.17, f32[256,256]{1,0:T(8,128)} %x_ref.3), custom_call_target="tpu_custom_call" | custom-call | tf_op jit(solution)/shard_map/gather_rows/pallas_call | solution.py:117
  16.8 16.6 %forward_tiles.1 = (f32[64,264,128]{2,1,0:T(8,128)}, s32[1024]{0:T(1024)}) custom-call(s32[1,192]{1,0:T(1,128)} %bitcast.21, s32[1,192]{1,0:T(1,128)} %bitcast.18, s32[2,192]{1,0:T(2,128)} %get-tuple-element.21.keys, s32[1]{0:T(128)} %bitcast.10.count, f32[1024,256]{1,0:T(8,128)} %get-tuple-element.22.x_ref, f32[192,128,128]{2,1,0:T(8,128)} %bitcast.11), custom_call_target="tpu_custom_call" | custom-call | flops 4831838208 | bytes 22000000 | tf_op jit(solution)/shard_map/forward_tiles/pallas_call | solution.py:216
  33.4 94.7 %exchange.1 = (f32[256,256]{1,0:T(8,128)}, f32[256,256]{1,0:T(8,128)}, f32[4,2,4,2,256,128]{5,4,3,2,1,0:T(8,128)}, f32[40,128]{1,0:T(8,128)}, f32[1024,256]{1,0:T(8,128)}) custom-call(s32[1024]{0:T(1024)} %get-tuple-element.23.plan, f32[4,4,2,2,264,128]{5,4,3,2,1,0:T(8,128)} %bitcast.14, f32[256,256]{1,0:T(8,128)} %x_ref.3, f32[256,256]{1,0:T(8,128)} %ws_ref.1, ...), custom_call_target="tpu_custom_call" | custom-call | tf_op jit(solution)/shard_map/exchange/pallas_call | solution.py:659
  128.0 2.6 %backward_rest.1.back_hbm = f32[1024,256]{1,0:T(8,128)} custom-call(s32[1024]{0:T(1024)} %get-tuple-element.23.plan, s32[1,192]{1,0:T(1,128)} %bitcast.19, s32[2,192]{1,0:T(2,128)} %get-tuple-element.21.keys, f32[64,256,128]{2,1,0:T(8,128)} %bitcast.15, f32[192,128,128]{2,1,0:T(8,128)} %bitcast.13, f32[1024,256]{1,0:T(8,128)} %get-tuple-element.28.back_ref), custom_call_target="tpu_custom_call" | custom-call | tf_op jit(solution)/shard_map/backward_rest/pallas_call | solution.py:761
  130.6 22.1 %scatter_rows.1 = (f32[256,256]{1,0:T(8,128)}, f32[2,4,4,40,128]{4,3,2,1,0:T(8,128)}) custom-call(f32[1024,256]{1,0:T(8,128)} %backward_rest.1.back_hbm, f32[40,128]{1,0:T(8,128)} %get-tuple-element.29.part_ref), custom_call_target="tpu_custom_call" | custom-call | tf_op jit(solution)/shard_map/scatter_rows/pallas_call | solution.py:852
  152.8 2.3 %finish.1 = (f32[256,256]{1,0:T(8,128)}, f32[256,256]{1,0:T(8,128)}, f32[256,256]{1,0:T(8,128)}, f32[256,256]{1,0:T(8,128)}, f32[1,256]{1,0:T(1,128)}) custom-call(f32[256,256]{1,0:T(8,128)} %get-tuple-element.25.kept, f32[256,256]{1,0:T(8,128)} %get-tuple-element.26.direct, f32[256,256]{1,0:T(8,128)} %get-tuple-element.30.back, f32[1280,128]{1,0:T(8,128)} %bitcast.16), custom_call_target="tpu_custom_call" | custom-call | tf_op jit(solution)/shard_map/finish/pallas_call | solution.py:890
